TPU v7x, 256 devices: a whole 4x4x8 slice. The times are simulated.
256 devices in a mesh: pts: 16 (over z_hi, x, core), cen: 16 (over y, z_lo).
Axes of the slice: x: 4, y: 4, z: 8 (z_hi: 2, z_lo: 4; z = z_hi * 4 + z_lo), core: 2. Of those that a mesh axis runs over, the one named last changes fastest.
Arguments:
- sample_vectors: float32 [12288, 1024], P('pts'), may hold values from -4 to 4
- centroids: float32 [1024, 16384], P(None, 'cen'), may hold values from -1 to 1
Outputs:
- responsibilities: float32 [12288, 16384], P('pts', 'cen')
- new_centroids: float32 [1024, 16384], P('pts', 'cen')
All inputs are finite; a program needn't handle non-finite values.
Results may differ from a plain program's by a relative error of at most 0.00075.
Values sent between devices are 32-bit elements; how exact they have to be, the bound alone decides.
No kernel may reach another device: no remote copies, remote signals or barrier semaphores. Data moves between devices by JAX's collectives and lax.ppermute only.
A program may use at most 128 MiB of HBM per device.

v0:
```python
import functools

import jax
import jax.numpy as jnp
from jax import lax
from jax.experimental import pallas as pl
from jax.experimental.pallas import tpu as pltpu
from jax.sharding import PartitionSpec as P

F32 = jnp.float32
BF16 = jnp.bfloat16
PAD = 8
MIB = 1 << 20
CORE, XA, XB, ZG = 1, 2, 6, 8
X_PEERS = (2, 4, 6)
COLORS = ((CORE, XA, XB), (CORE, XB, XA))
COST = 0.1


def split(v):
    hi = v.astype(BF16)
    return hi, (v - hi.astype(F32)).astype(BF16)


def dot3(ah, al, bh, bl):
    dot = functools.partial(jnp.dot, preferred_element_type=F32)
    return dot(ah, bh) + (dot(ah, bl) + dot(al, bh))


def swap(v, g):
    return lax.ppermute(v, "pts", [(i, i ^ g) for i in range(lax.axis_size("pts"))])


def relative_blocks(gens):
    out = [0]
    for g in reversed(gens):
        out = out + [r ^ g for r in out]
    return out


def params(mib):
    return pltpu.CompilerParams(vmem_limit_bytes=mib * MIB)


def cost(flops, nbytes):
    return pl.CostEstimate(
        flops=int(flops * COST), bytes_accessed=int(nbytes * COST), transcendentals=0
    )


def far_memory(*arrays):
    out = [pltpu.with_memory_space_constraint(a, pltpu.HBM) for a in arrays]
    return out[0] if len(out) == 1 else out


def near_memory(*arrays):
    return [pltpu.with_memory_space_constraint(a, pltpu.VMEM) for a in arrays]


ANY = pl.BlockSpec(memory_space=pl.ANY)
SMALL = pl.BlockSpec(memory_space=pltpu.SMEM)
NEAR = pl.BlockSpec(memory_space=pltpu.VMEM)


def whole(a):
    return pl.BlockSpec(a.shape, lambda i, s: (0,) * len(a.shape))


def softmax_part(raw_ref, half_norm, e_ref, at):
    logits = (raw_ref[...] - half_norm) * 10.0
    top = jnp.max(logits, axis=1, keepdims=True)
    expo = jnp.exp(logits - top)
    total = jnp.sum(expo, axis=1, keepdims=True)
    e_ref[at, :] = expo
    row = lambda v: jnp.broadcast_to(v, (v.shape[0], 128)).T[0:1, :]
    return row(top), row(total)


def tiled3(tiles, product, finish, raws):
    for i in range(tiles + 1):
        if i < tiles:
            raws[i % 2][...] = product(i)
        if i > 0:
            finish(i - 1, raws[(i - 1) % 2])


def tiled(tiles, product, finish, raws):
    @pl.loop(0, tiles)
    def _(i):
        raws[0][...] = product(i)
        finish(i, raws[0])


def put_stats(stats, stat_ref, all_ref, at):
    for i, v in enumerate(stats):
        stat_ref[i : i + 1, at] = v
        all_ref[:, i : i + 1, at] = jnp.broadcast_to(v[None], (all_ref.shape[0], *v.shape))


def first_kernel(
    me_ref,
    at_ref,
    pin_ref,
    x_ref,
    c_ref,
    e_ref,
    stat_ref,
    all_ref,
    xh_ref,
    xl_ref,
    th_ref,
    tl_ref,
    xs,
    cs,
    ch,
    cl,
    raw0,
    raw1,
    sems,
):
    tile = raw0.shape[0]
    tiles = x_ref.shape[0] // tile
    chunks = sems.shape[0] - tiles
    step = c_ref.shape[0] // chunks
    c_at = [pl.ds(j * step, step) for j in range(chunks)]
    x_at = [pl.ds(j * tile, tile) for j in range(tiles)]
    c_in = [
        pltpu.make_async_copy(c_ref.at[at, :], cs.at[at, :], sems.at[j])
        for j, at in enumerate(c_at)
    ]
    x_in = [
        pltpu.make_async_copy(x_ref.at[at, :], xs.at[at, :], sems.at[chunks + j])
        for j, at in enumerate(x_at)
    ]
    for copy in c_in + x_in:
        copy.start()
    total = jnp.zeros((1, cs.shape[1]), F32)
    def arrived(j, total):
        at = pl.ds(pl.multiple_of(j * step, step), step)
        pltpu.make_async_copy(c_ref.at[at, :], cs.at[at, :], sems.at[j]).wait()
        v = cs[at, :]
        ch[at, :], cl[at, :] = split(v)
        return total + jnp.sum(v * v, axis=0, keepdims=True)

    total = lax.fori_loop(0, chunks, arrived, total)
    half_norm = 0.5 * total

    def product(i):
        at = x_at[i]
        x_in[i].wait()
        x = xs[at, :]
        hi, lo = split(x)
        xh_ref[at, :] = hi
        xl_ref[at, :] = lo
        th_ref[:, at], tl_ref[:, at] = split(x.T)
        return dot3(hi, lo, ch[...], cl[...])

    def finish(i, raw):
        put_stats(softmax_part(raw, half_norm, e_ref, x_at[i]), stat_ref, all_ref, x_at[i])

    tiled3(tiles, product, finish, (raw0, raw1))


def first_step(me, at, pin, x, c, copies, tile=256, chunks=8):
    n, d = x.shape
    k = c.shape[1]
    return pl.pallas_call(
        first_kernel,
        in_specs=[SMALL, SMALL, ANY, ANY, ANY],
        out_specs=[NEAR] * 7,
        out_shape=[
            pltpu.VMEM((n, k), F32),
            jax.ShapeDtypeStruct((2, n), F32),
            jax.ShapeDtypeStruct((copies, 2, n), F32),
            pltpu.VMEM((n, d), BF16),
            pltpu.VMEM((n, d), BF16),
            pltpu.VMEM((d, n), BF16),
            pltpu.VMEM((d, n), BF16),
        ],
        scratch_shapes=[
            pltpu.VMEM((n, d), F32),
            pltpu.VMEM((d, k), F32),
            pltpu.VMEM((d, k), BF16),
            pltpu.VMEM((d, k), BF16),
            pltpu.VMEM((tile, k), F32),
            pltpu.VMEM((tile, k), F32),
            pltpu.SemaphoreType.DMA((chunks + n // tile,)),
        ],
        compiler_params=params(36),
        cost_estimate=cost(20 * 6 * n * d * k, 4 * (2 * n * d + d * k + n * k)),
        name="first_logits",
    )(me, at, pin, *far_memory(x, c))


def far_kernel(at_ref, *refs):
    pieces, (xh_ref, xl_ref, th_ref, tl_ref) = refs[:4], refs[4:]
    width = pieces[0].shape[1]
    for shift, piece in enumerate(pieces):
        quarter = lax.rem(at_ref[3] - shift + 4, 4)
        at = pl.ds(pl.multiple_of(quarter * width, width), width)
        v = piece[...]
        xh_ref[:, at], xl_ref[:, at] = split(v)
        th_ref[at, :], tl_ref[at, :] = split(v.T)


def far_points(at, pieces):
    n, width = pieces[0].shape
    d = width * len(pieces)
    return pl.pallas_call(
        far_kernel,
        in_specs=[SMALL] + [NEAR] * len(pieces),
        out_specs=[NEAR] * 4,
        out_shape=[pltpu.VMEM(s, BF16) for s in ((n, d), (n, d), (d, n), (d, n))],
        compiler_params=params(16),
        cost_estimate=cost(4 * n * d, 12 * n * d),
        name="far_points",
    )(at, *pieces)


def slice_kernel(at_ref, pin_ref, x_ref, out_ref):
    out_ref[...] = x_ref[...]


def own_piece(x, at):
    n, size = x.shape[0], x.shape[1] // 8
    return pl.pallas_call(
        lambda at_ref, x_ref, out_ref: slice_kernel(at_ref, None, x_ref, out_ref),
        grid_spec=pltpu.PrefetchScalarGridSpec(
            num_scalar_prefetch=1,
            grid=(1,),
            in_specs=[pl.BlockSpec((n, size), lambda i, s: (0, s[0]))],
            out_specs=pl.BlockSpec((n, size), lambda i, s: (0, 0)),
        ),
        out_shape=jax.ShapeDtypeStruct((n, size), F32),
        compiler_params=params(8),
        cost_estimate=cost(1, 8 * n * size),
        name="own_piece",
    )(at, far_memory(x))


def couple_kernel(at_ref, pin_ref, mine_ref, other_ref, out_ref):
    width = mine_ref.shape[1]
    side = at_ref[0] & 1
    out_ref[:, pl.ds(pl.multiple_of(side * width, width), width)] = mine_ref[...]
    out_ref[:, pl.ds(pl.multiple_of((1 - side) * width, width), width)] = other_ref[...]


def couple(at, pin, mine, other):
    n, width = mine.shape
    return pl.pallas_call(
        couple_kernel,
        in_specs=[SMALL, ANY, NEAR, NEAR],
        out_specs=NEAR,
        out_shape=jax.ShapeDtypeStruct((n, 2 * width), F32),
        compiler_params=params(4),
        cost_estimate=cost(1, 16 * n * width),
        name="couple",
    )(at, pin, mine, other)


def old_block(c, me, rows, width, pin):
    return pl.pallas_call(
        slice_kernel,
        grid_spec=pltpu.PrefetchScalarGridSpec(
            num_scalar_prefetch=1,
            grid=(2,),
            in_specs=[
                ANY,
                pl.BlockSpec((rows, width), lambda b, s: ((s[0] & 7) + 8 * b, s[0] // 8)),
            ],
            out_specs=pl.BlockSpec((rows, width), lambda b, s: (b, 0)),
        ),
        out_shape=jax.ShapeDtypeStruct((2 * rows, width), F32),
        compiler_params=params(4),
        cost_estimate=cost(1, 16 * rows * width),
        name="old_block",
    )(me, pin, far_memory(c))


def spread(me, sides, ch, cl):
    total = jnp.zeros((1, ch.shape[1]), F32)
    for side, ref in sides:
        rows = ref.shape[0] // 8

        def body(j, total):
            v = ref[pl.ds(pl.multiple_of(j * rows, rows), rows), :]
            hi, lo = split(v)
            at = (((me ^ (j // 2 * 2) ^ side) & 7) + 8 * (j % 2)) * rows
            at = pl.ds(pl.multiple_of(at, rows), rows)
            ch[at, :] = hi
            cl[at, :] = lo
            return total + jnp.sum(v * v, axis=0, keepdims=True)

        total = lax.fori_loop(0, 8, body, total)
    return 0.5 * total


def own_kernel(me_ref, mine_ref, other_ref, xh, xl, e_ref, stat_ref, ch, cl, norm, raw0, raw1):
    me = me_ref[0]
    half_norm = spread(
        me, ((0, mine_ref), (CORE, other_ref)), ch, cl
    )
    norm[...] = jnp.broadcast_to(half_norm, norm.shape)
    tile = raw0.shape[0]

    def finish(i, raw):
        at = pl.ds(pl.multiple_of(i * tile, tile), tile)
        for j, v in enumerate(softmax_part(raw, half_norm, e_ref, at)):
            stat_ref[j : j + 1, at] = v

    product = lambda i: dot3(
        xh[pl.ds(pl.multiple_of(i * tile, tile), tile), :], xl[pl.ds(pl.multiple_of(i * tile, tile), tile), :], ch[...], cl[...]
    )
    tiled(xh.shape[0] // tile, product, finish, (raw0, raw1))


def own_logits(me, mine, other, near, tile=256):
    n, d = near[0].shape
    k = mine.shape[1]
    return pl.pallas_call(
        own_kernel,
        in_specs=[SMALL] + [NEAR] * 4,
        out_specs=[NEAR] * 5,
        out_shape=[
            pltpu.VMEM((n, k), F32),
            jax.ShapeDtypeStruct((2, n), F32),
            pltpu.VMEM((d, k), BF16),
            pltpu.VMEM((d, k), BF16),
            pltpu.VMEM((8, k), F32),
        ],
        scratch_shapes=[pltpu.VMEM((tile, k), F32)] * 2,
        compiler_params=params(20),
        cost_estimate=cost(6 * n * d * k, 4 * (n * d + d * k + n * k)),
        name="own_logits",
    )(me, mine, other, *near)


def far_logits_kernel(me_ref, ch, cl, norm, own_ref, xh, xl, e_ref, stat_ref, raw0, raw1):
    tile = raw0.shape[0]
    n = own_ref.shape[1]
    z = me_ref[0] // 8
    stat_ref[:, pl.ds(pl.multiple_of(z * n, n), n)] = own_ref[...]

    def finish(i, raw):
        at = pl.ds(pl.multiple_of((1 - z) * n + i * tile, tile), tile)
        stats = softmax_part(raw, norm[0:1, :], e_ref, pl.ds(pl.multiple_of(i * tile, tile), tile))
        for j, v in enumerate(stats):
            stat_ref[j : j + 1, at] = v

    product = lambda i: dot3(
        xh[pl.ds(pl.multiple_of(i * tile, tile), tile), :], xl[pl.ds(pl.multiple_of(i * tile, tile), tile), :], ch[...], cl[...]
    )
    tiled(n // tile, product, finish, (raw0, raw1))


def far_logits(me, ch, cl, norm, own, far, tile=256):
    n, d = far[0].shape
    k = ch.shape[1]
    return pl.pallas_call(
        far_logits_kernel,
        in_specs=[SMALL] + [NEAR] * 6,
        out_specs=[NEAR] * 2,
        out_shape=[pltpu.VMEM((n, k), F32), jax.ShapeDtypeStruct((2, 2 * n), F32)],
        scratch_shapes=[pltpu.VMEM((tile, k), F32)] * 2,
        compiler_params=params(16),
        cost_estimate=cost(6 * n * d * k, 4 * (n * d + d * k + n * k)),
        name="far_logits",
    )(me, ch, cl, norm, own, *far)


def merge_kernel(pin_ref, mine_ref, other_ref, out_ref):
    top = jnp.maximum(mine_ref[0:1, :], other_ref[0:1, :])
    total = sum(ref[1:2, :] * jnp.exp(ref[0:1, :] - top) for ref in (mine_ref, other_ref))
    for i, v in enumerate((top, total)):
        out_ref[:, i : i + 1, :] = jnp.broadcast_to(v[None], (out_ref.shape[0], *v.shape))


def merge(pin, mine, other, copies):
    return pl.pallas_call(
        merge_kernel,
        in_specs=[ANY, NEAR, NEAR],
        out_specs=NEAR,
        out_shape=jax.ShapeDtypeStruct((copies, *mine.shape), F32),
        compiler_params=params(4),
        cost_estimate=cost(copies * mine.size, 8 * copies * mine.size),
        name="merge",
    )(pin, mine, other)


def row_scale(own, everyone):
    tops = everyone[:, 0, :]
    top = jnp.max(tops, axis=0, keepdims=True)
    total = jnp.sum(everyone[:, 1, :] * jnp.exp(tops - top), axis=0, keepdims=True)
    scale = jnp.exp(own[0:1, :] - top) / total
    return jnp.broadcast_to(scale, (128, scale.shape[1])).T[:, 0:1]


def permuted(order, low, ref, out):
    rows = ref.shape[0] // (2 * len(order))
    for j, r in enumerate(order):
        for b in range(2):
            at = pl.ds(pl.multiple_of(((low ^ r) + 8 * b) * rows, rows), rows)
            out[(2 * j + b) * rows : (2 * j + b + 1) * rows, :] = ref[at, :]


def emit(m, w, keep_ref, send_ref, at):
    half = m.shape[0] // 2
    mass = jnp.broadcast_to(jnp.sum(w, axis=0, keepdims=True), (PAD, w.shape[1]))
    keep_ref[0:half, at] = m[:half]
    send_ref[0:half, at] = m[half:]
    keep_ref[half : half + PAD, at] = mass
    send_ref[half : half + PAD, at] = mass


def first_moment_kernel(
    order, color, me_ref, pin_ref, own_ref, all_ref, th_ref, tl_ref, e_ref, keep_ref, send_ref, ph, pt
):
    low, z = me_ref[0] & 7, me_ref[0] // 8
    permuted(order, low, th_ref, ph)
    permuted(order, low, tl_ref, pt)
    scale = row_scale(own_ref[...], all_ref[...])
    width = e_ref.shape[1] // 4
    for h in range(2):
        column = pl.multiple_of((2 * (z ^ h) + color) * width, width)
        w = e_ref[:, pl.ds(column, width)] * scale
        wh, wl = split(w)
        m = dot3(ph[...], pt[...], wh, wl)
        emit(m, w, keep_ref, send_ref, slice(h * width, (h + 1) * width))


def first_moments(me, pin, own, everyone, th, tl, e, color, order):
    d, n = th.shape
    width = e.shape[1] // 4
    shape = jax.ShapeDtypeStruct((d // 2 + PAD, 2 * width), F32)
    return pl.pallas_call(
        functools.partial(first_moment_kernel, order, color),
        in_specs=[SMALL, ANY] + [NEAR] * 5,
        out_specs=[NEAR, NEAR],
        out_shape=[shape, shape],
        scratch_shapes=[pltpu.VMEM((d, n), BF16), pltpu.VMEM((d, n), BF16)],
        compiler_params=params(20),
        cost_estimate=cost(12 * d * n * width, 4 * (d * n + 2 * n * width + 2 * d * width)),
        name="first_moments",
    )(me, pin, own, everyone, th, tl, e)


def next_moment_kernel(
    order, color, me_ref, pin_ref, own, everyone, oh, ol, gh, gl, e0, e1, keep_ref, send_ref, ph, pt
):
    low, z = me_ref[0] & 7, me_ref[0] // 8
    n = e0.shape[0]
    width = e0.shape[1] // 2
    m = w_all = None
    for h, (th, tl, e) in enumerate(((oh, ol, e0), (gh, gl, e1))):
        at = pl.ds(pl.multiple_of((z ^ h) * n, n), n)
        permuted(order, low, th, ph)
        permuted(order, low, tl, pt)
        w = e[:, color * width : (color + 1) * width] * row_scale(own[:, at], everyone[:, :, at])
        wh, wl = split(w)
        part = dot3(ph[...], pt[...], wh, wl)
        m, w_all = (part, w) if m is None else (m + part, w_all + w)
    emit(m, w_all, keep_ref, send_ref, slice(None))


def next_moments(me, pin, own, everyone, near, far, e_own, e_far, color, order):
    d, n = near[0].shape
    width = e_own.shape[1] // 2
    shape = jax.ShapeDtypeStruct((d // 2 + PAD, width), F32)
    return pl.pallas_call(
        functools.partial(next_moment_kernel, order, color),
        in_specs=[SMALL, ANY] + [NEAR] * 8,
        out_specs=[NEAR, NEAR],
        out_shape=[shape, shape],
        scratch_shapes=[pltpu.VMEM((d, n), BF16)] * 2,
        compiler_params=params(20),
        cost_estimate=cost(12 * d * n * width, 4 * (2 * d * n + 2 * n * width + d * width)),
        name="next_moments",
    )(me, pin, own, everyone, *near, *far, e_own, e_far)


def relay_kernel(pin_ref, in_ref, out_ref):
    pass


def relay(a, pin):
    return pl.pallas_call(
        relay_kernel,
        in_specs=[ANY, ANY],
        out_specs=ANY,
        out_shape=jax.ShapeDtypeStruct(a.shape, a.dtype),
        input_output_aliases={1: 0},
        compiler_params=params(4),
        cost_estimate=cost(1, 1),
        name="relay",
    )(pin, a)


def chain(kernel, name, ins, shapes, pins=()):
    size = sum(a.size for a in ins)
    return pl.pallas_call(
        kernel,
        in_specs=[ANY] * len(pins) + [NEAR] * len(ins),
        out_shape=[jax.ShapeDtypeStruct(shape, F32) for shape in shapes],
        compiler_params=params(16),
        cost_estimate=cost(size, 8 * size),
        name=name,
    )(*pins, *ins)


def fold_kernel(pins, *refs):
    refs = refs[pins:]
    count = len(refs) // 4
    for u in range(count):
        keep, recv = refs[2 * u : 2 * u + 2]
        out, send = refs[2 * (count + u) : 2 * (count + u) + 2]
        half = (keep.shape[0] - PAD) // 2
        out[0:half, :] = keep[0:half, :] + recv[0:half, :]
        send[0:half, :] = keep[half : 2 * half, :] + recv[half : 2 * half, :]
        mass = keep[2 * half :, :] + recv[2 * half :, :]
        out[half:, :] = mass
        send[half:, :] = mass


def fold(ins, *pins):
    shapes = []
    for keep, _ in ins:
        shapes += [((keep.shape[0] - PAD) // 2 + PAD, keep.shape[1])] * 2
    kernel = functools.partial(fold_kernel, len(pins))
    flat = chain(kernel, "fold", [a for pair in ins for a in pair], shapes, pins)
    return [(flat[2 * i], flat[2 * i + 1]) for i in range(len(ins))]


def part_kernel(*refs):
    ins, (out, send) = refs[:-2], refs[-2:]
    for u in range(len(ins) // 2):
        keep, recv = ins[2 * u : 2 * u + 2]
        half = keep.shape[1] // 2
        cols = slice(u * half, (u + 1) * half)
        out[:, cols] = keep[:, 0:half] + recv[:, 0:half]
        send[:, cols] = keep[:, half:] + recv[:, half:]


def part(ins):
    rows, width = ins[0][0].shape
    shape = (rows, width // 2 * len(ins))
    return chain(part_kernel, "part", [a for pair in ins for a in pair], [shape] * 2)


def update_kernel(pins, *refs):
    keep, recv, old, out = refs[pins:]
    rows = old.shape[0]
    mass = keep[rows : rows + 1, :] + recv[rows : rows + 1, :] + 1.0
    out[...] = (keep[0:rows, :] + recv[0:rows, :] + old[...]) / mass


def update(keep, recv, old, *pins):
    kernel = functools.partial(update_kernel, len(pins))
    return chain(kernel, "update", [keep, recv, old], [old.shape], pins)[0]


def column_kernel(pins, *refs):
    refs = refs[pins:]
    rows = refs[0].shape[0]
    for i, ref in enumerate(refs[:-1]):
        refs[-1][i * rows : (i + 1) * rows, :] = ref[...]


def column(pieces, *pins):
    rows, width = pieces[0].shape
    kernel = functools.partial(column_kernel, len(pins))
    return chain(kernel, "column", pieces, [(rows * len(pieces), width)], pins)[0]


def last_kernel(me_ref, old, *refs):
    ins, (mine_ref, theirs_ref) = refs[:-2], refs[-2:]
    z = me_ref[0] // 8
    rows = old.shape[0]
    for u in range(len(ins) // 2):
        keep, recv = ins[2 * u : 2 * u + 2]
        cols = slice(u * keep.shape[1], (u + 1) * keep.shape[1])
        mass = keep[rows : rows + 1, :] + recv[rows : rows + 1, :] + 1.0
        for out, which in ((mine_ref, z), (theirs_ref, 1 - z)):
            at = pl.ds(pl.multiple_of(which * (rows // 2), rows // 2), rows // 2)
            out[:, cols] = (keep[at, :] + recv[at, :] + old[at, cols]) / mass


def last_update(me, ins, old):
    rows, width = old.shape
    shape = jax.ShapeDtypeStruct((rows // 2, width), F32)
    flat = [a for pair in ins for a in pair]
    return pl.pallas_call(
        last_kernel,
        in_specs=[SMALL] + [NEAR] * (1 + len(flat)),
        out_specs=[NEAR] * 2,
        out_shape=[shape, shape],
        compiler_params=params(16),
        cost_estimate=cost(8 * rows * width, 32 * rows * width),
        name="last_update",
    )(me, old, *flat)


def weights_kernel(
    me_ref,
    own_ref,
    all_ref,
    e_ref,
    xh_ref,
    xl_ref,
    mine_ref,
    other_ref,
    out_ref,
    tick_ref,
    ch,
    cl,
    norm,
):
    me = me_ref[0]
    z = me // 8

    @pl.when(pl.program_id(0) == 0)
    def _():
        sides = (0, mine_ref), (CORE, other_ref)
        norm[...] = jnp.broadcast_to(spread(me, sides, ch, cl), norm.shape)

    tops = all_ref[:, 0, :]
    top = jnp.max(tops, axis=0, keepdims=True)
    total = jnp.sum(all_ref[:, 1, :] * jnp.exp(tops - top), axis=0, keepdims=True)
    width = e_ref.shape[1]
    column = lambda v: jnp.broadcast_to(v, (128, v.shape[1])).T[:, 0:1]
    here = pl.ds(pl.multiple_of(z * width, width), width)
    there = pl.ds(pl.multiple_of((1 - z) * width, width), width)
    out_ref[:, here] = e_ref[...] * column(jnp.exp(own_ref[0:1, :] - top) / total)
    raw = dot3(xh_ref[...], xl_ref[...], ch[...], cl[...])
    logits = (raw - norm[0:1, :]) * 10.0
    out_ref[:, there] = jnp.exp(logits - column(top)) * column(1.0 / total)
    tick_ref[...] = norm[:, 0:128]


def final_weights(me, own, everyone, e_own, near, mine, other, tile=256):
    n, width = e_own.shape
    d = near[0].shape[1]
    t = n // tile
    rows = pl.BlockSpec((tile, d), lambda i, s: (i, 0))
    return pl.pallas_call(
        weights_kernel,
        grid_spec=pltpu.PrefetchScalarGridSpec(
            num_scalar_prefetch=1,
            grid=(t,),
            in_specs=[
                pl.BlockSpec((2, tile), lambda i, s: (0, (s[0] // 8) * t + i)),
                pl.BlockSpec(
                    (everyone.shape[0], 2, tile), lambda i, s: (0, 0, (s[0] // 8) * t + i)
                ),
                pl.BlockSpec((tile, width), lambda i, s: (i, 0)),
                rows,
                rows,
                NEAR,
                NEAR,
            ],
            out_specs=[pl.BlockSpec((tile, 2 * width), lambda i, s: (i, 0)), NEAR],
            scratch_shapes=[
                pltpu.VMEM((d, width), BF16),
                pltpu.VMEM((d, width), BF16),
                pltpu.VMEM((8, width), F32),
            ],
        ),
        out_shape=[pltpu.HBM((n, 2 * width), F32), jax.ShapeDtypeStruct((8, 128), F32)],
        compiler_params=params(24),
        cost_estimate=cost(6 * n * width * d, 4 * (n * d + 3 * n * width + d * width)),
        name="weights",
    )(me, own, everyone, e_own, *near, mine, other)


def local(x, c):
    index = lax.axis_index("pts").astype(jnp.int32)
    me = index.reshape(1)
    place_cen = lax.axis_index("cen").astype(jnp.int32)
    run, y = place_cen & 3, place_cen // 4
    at = jnp.stack([y * 2 + (run & 1), run >> 1, run, y])
    d, k = c.shape
    rows = d // 16
    cen = lax.axis_size("cen")
    along_y = lambda v, shift: lax.ppermute(
        v, "cen", [(j, (j + 4 * shift) % cen) for j in range(cen)]
    )

    piece = own_piece(x, at)
    e, stats, copies, xh, xl, th, tl = first_step(me, at, piece, x, c, cen)
    piece = swap(piece, ZG)
    everyone = lax.all_to_all(copies, "cen", 0, 0)
    orders = [relative_blocks(gens) for gens in COLORS]
    swapped = lambda units, step: [
        (keep, swap(send, gens[step])) for gens, (keep, send) in zip(COLORS, units)
    ]
    units, pin = [], piece
    for u, order in enumerate(orders):
        units.append(first_moments(me, pin, stats, everyone, th, tl, e, u, order))
        pin = units[-1][1]
    old = old_block(c, me, rows, k // 2, pin)
    other = lax.ppermute(relay(piece, units[0][1]), "cen", [(j, j ^ 1) for j in range(cen)])
    quarter = couple(at, old, piece, other)
    units = fold(swapped(units, 0))
    units = fold(swapped(units, 1), quarter)
    quarters = [quarter] + [along_y(quarter, shift) for shift in (1, 2, 3)]
    keep, send = part(swapped(units, 2))
    share = update(keep, swap(send, ZG), old)
    joint = swap(share, ZG)
    mine = column([share] + [swap(share, mask) for mask in X_PEERS], *quarters[1:])
    fh, fl, gh, gl = far_points(at, quarters)
    e_own, stats, ch, cl, norm = own_logits(me, mine, swap(mine, CORE), (xh, xl))
    e_far, stats = far_logits(me, ch, cl, norm, stats, (fh, fl))
    everyone = lax.all_to_all(merge(joint, stats, swap(stats, ZG), cen), "cen", 0, 0)
    joint = relay(joint, everyone)
    peers = [joint] + [swap(joint, mask) for mask in X_PEERS]
    units, pin = [], everyone
    for u, order in enumerate(orders):
        units.append(
            next_moments(me, pin, stats, everyone, (th, tl), (gh, gl), e_own, e_far, u, order)
        )
        pin = units[-1][1]
    far_mine = column(peers, pin)
    units = fold(swapped(units, 0))
    units = fold(swapped(units, 1))
    far_other = swap(far_mine, CORE)
    weights, tick = final_weights(me, stats, everyone, e_own, (xh, xl), far_mine, far_other)
    mine, theirs = last_update(me, swapped(units, 2), share)
    return weights, place(me, tick, mine, swap(theirs, ZG))


def place_kernel(me_ref, pin_ref, mine_ref, other_ref, out_ref):
    z = me_ref[0] // 8
    width = mine_ref.shape[1]
    out_ref[:, pl.ds(pl.multiple_of(z * width, width), width)] = mine_ref[...]
    out_ref[:, pl.ds(pl.multiple_of((1 - z) * width, width), width)] = other_ref[...]


def place(me, pin, mine, other):
    rows, width = mine.shape
    return pl.pallas_call(
        place_kernel,
        in_specs=[SMALL, ANY, NEAR, NEAR],
        out_specs=NEAR,
        out_shape=jax.ShapeDtypeStruct((rows, 2 * width), F32),
        compiler_params=params(4),
        cost_estimate=cost(1, 16 * rows * width),
        name="place",
    )(me, pin, mine, other)


def solution(mesh):
    placed = (P("pts", None), P(None, "cen"))
    return jax.shard_map(
        local,
        mesh=mesh,
        in_specs=placed,
        out_specs=(P("pts", "cen"), P("pts", "cen")),
        check_vma=False,
    )
```

profile of v0, /device:TPU:8, one launch (start us, length us, event | category | flops | bytes accessed | tf_op | source)
XLA Modules:
  0.0 178.1 jit_solution(693123984753860175)
XLA Ops:
  0.7 1.6 own_piece.1.pin_ref
  2.3 7.3 %collective-permute-start = (f32[768,128]{1,0:T(8,128)S(1)}, f32[768,128]{1,0:T(8,128)S(1)}, u32[]{:S(2)}, u32[]{:S(2)}) collective-permute-start(f32[768,128]{1,0:T(8,128)S(1)} %own_piece.1.pin_ref), channel_id=1, source_target_pairs={{0,128},{16,144},{32,160},{48,176},{64,192},{80,208},{96,224},{112... | collective-permute-start | bytes 1179656 | tf_op jit(solution)/shard_map/ppermute | solution.py:31
  9.6 9.2 %first_logits.1 = (f32[768,1024]{1,0:T(8,128)S(1)}, f32[2,768]{1,0:T(2,128)S(1)}, f32[16,2,768]{2,1,0:T(2,128)S(1)}, bf16[768,1024]{1,0:T(8,128)(2,1)S(1)}, bf16...) custom-call(s32[1]{0:T(128)} %bitcast.me_ref.at_ref, ...), custom_call_target="tpu_custom_call" | custom-call | flops 9663676416 | bytes 1363148 | tf_op jit(solution)/shard_map/first_logits/pallas_call | solution.py:167
  18.8 13.0 %all_to_all.10.all_ref = f32[16,2,768]{2,1,0:T(2,128)S(1)} all-to-all(f32[16,2,768]{2,1,0:T(2,128)S(1)} %get-tuple-element.51), channel_id=1, replica_groups=mesh['pts'=16,'cen'=16] {'cen'}, dimensions={0} | all-to-all | bytes 196608 | tf_op jit(solution)/shard_map/all_to_all | solution.py:690
  31.8 2.8 %first_moments.2 = (f32[520,512]{1,0:T(8,128)S(1)}, f32[520,512]{1,0:T(8,128)S(1)}) custom-call(s32[1]{0:T(128)} %bitcast.me_ref.at_ref, f32[768,128]{1,0:T(8,128)S(1)} %collective-permute-done.pin_ref.mine_ref, f32[2,768]{1,0:T(2,128)S(1)} %get-tuple-element.50.own_ref, f32[16,2,768]{2,1,0:T(2,128)S(1)} %all_to_all.10.all_ref, ...), custom_call_target="tpu_custom_call" | custom-call | flops 241591904 | bytes 681574 | tf_op jit(solution)/shard_map/first_moments/pallas_call | solution.py:435
  34.7 2.8 %first_moments.3 = (f32[520,512]{1,0:T(8,128)S(1)}, f32[520,512]{1,0:T(8,128)S(1)}) custom-call(s32[1]{0:T(128)} %bitcast.me_ref.at_ref, f32[520,512]{1,0:T(8,128)S(1)} %get-tuple-element.55.pin_ref, f32[2,768]{1,0:T(2,128)S(1)} %get-tuple-element.50.own_ref, f32[16,2,768]{2,1,0:T(2,128)S(1)} %all_to_all.10.all_ref, ...), custom_call_target="tpu_custom_call" | custom-call | flops 241591904 | bytes 681574 | tf_op jit(solution)/shard_map/first_moments/pallas_call | solution.py:435
  38.5 1.9 %collective-permute-done.6.refs_3_ = f32[520,512]{1,0:T(8,128)S(1)} collective-permute-done((f32[520,512]{1,0:T(8,128)S(1)}, f32[520,512]{1,0:T(8,128)S(1)}, u32[]{:S(2)}, u32[]{:S(2)}) %collective-permute-start.6) | collective-permute-done | bytes 1064992 | tf_op jit(solution)/shard_map/ppermute | solution.py:31
  40.6 1.8 %collective-permute-start.7 = (f32[264,512]{1,0:T(8,128)S(1)}, f32[264,512]{1,0:T(8,128)S(1)}, u32[]{:S(2)}, u32[]{:S(2)}) collective-permute-start(f32[264,512]{1,0:T(8,128)S(1)} %get-tuple-element.60), channel_id=1, source_target_pairs={{0,32},{16,48},{32,0},{48,16},{64,96},{80,112},{96,64},{112,80},{1... | collective-permute-start | bytes 1622024 | tf_op jit(solution)/shard_map/ppermute | solution.py:31
  42.4 2.1 %collective-permute-start.8 = (f32[264,512]{1,0:T(8,128)S(1)}, f32[264,512]{1,0:T(8,128)S(1)}, u32[]{:S(2)}, u32[]{:S(2)}) collective-permute-start(f32[264,512]{1,0:T(8,128)S(1)} %get-tuple-element.62), channel_id=1, source_target_pairs={{0,96},{16,112},{32,64},{48,80},{64,32},{80,48},{96,0},{112,16},{1... | collective-permute-start | bytes 1622024 | tf_op jit(solution)/shard_map/ppermute | solution.py:31
  44.5 1.0 old_block.1.pin_ref.refs_2_
  45.5 3.8 %collective-permute-done.1.other_ref = f32[768,128]{1,0:T(8,128)S(1)} collective-permute-done((f32[768,128]{1,0:T(8,128)S(1)}, f32[768,128]{1,0:T(8,128)S(1)}, u32[]{:S(2)}, u32[]{:S(2)}) %collective-permute-start.1) | collective-permute-done | bytes 393248 | tf_op jit(solution)/shard_map/ppermute | solution.py:700
  49.3 0.6 couple.1.refs_0_
  49.9 0.8 collective-permute-start.2
  50.6 4.8 %collective-permute-done.7.refs_2_ = f32[264,512]{1,0:T(8,128)S(1)} collective-permute-done((f32[264,512]{1,0:T(8,128)S(1)}, f32[264,512]{1,0:T(8,128)S(1)}, u32[]{:S(2)}, u32[]{:S(2)}) %collective-permute-start.7) | collective-permute-done | bytes 540704 | tf_op jit(solution)/shard_map/ppermute | solution.py:31
  55.4 2.4 %collective-permute-done.8.refs_4_ = f32[264,512]{1,0:T(8,128)S(1)} collective-permute-done((f32[264,512]{1,0:T(8,128)S(1)}, f32[264,512]{1,0:T(8,128)S(1)}, u32[]{:S(2)}, u32[]{:S(2)}) %collective-permute-start.8) | collective-permute-done | bytes 540704 | tf_op jit(solution)/shard_map/ppermute | solution.py:31
  58.0 2.2 %collective-permute-start.9 = (f32[136,512]{1,0:T(8,128)S(1)}, f32[136,512]{1,0:T(8,128)S(1)}, u32[]{:S(2)}, u32[]{:S(2)}) collective-permute-start(f32[136,512]{1,0:T(8,128)S(1)} %get-tuple-element.64), channel_id=1, source_target_pairs={{0,96},{16,112},{32,64},{48,80},{64,32},{80,48},{96,0},{112,16},{1... | collective-permute-start | bytes 835592 | tf_op jit(solution)/shard_map/ppermute | solution.py:31
  60.2 1.5 collective-permute-start.3
  61.6 1.3 collective-permute-start.4
  62.9 4.2 %collective-permute-done.9.refs_1_ = f32[136,512]{1,0:T(8,128)S(1)} collective-permute-done((f32[136,512]{1,0:T(8,128)S(1)}, f32[136,512]{1,0:T(8,128)S(1)}, u32[]{:S(2)}, u32[]{:S(2)}) %collective-permute-start.9) | collective-permute-done | bytes 278560 | tf_op jit(solution)/shard_map/ppermute | solution.py:31
  67.1 0.6 collective-permute-done.10.refs_3_
  67.8 3.0 %collective-permute-start.11 = (f32[136,512]{1,0:T(8,128)S(1)}, f32[136,512]{1,0:T(8,128)S(1)}, u32[]{:S(2)}, u32[]{:S(2)}) collective-permute-start(f32[136,512]{1,0:T(8,128)S(1)} %get-tuple-element.68), channel_id=1, source_target_pairs={{0,128},{16,144},{32,160},{48,176},{64,192},{80,208},{96,224},{112... | collective-permute-start | bytes 835592 | tf_op jit(solution)/shard_map/ppermute | solution.py:31
  70.8 9.3 %collective-permute-done.11.refs_1_ = f32[136,512]{1,0:T(8,128)S(1)} collective-permute-done((f32[136,512]{1,0:T(8,128)S(1)}, f32[136,512]{1,0:T(8,128)S(1)}, u32[]{:S(2)}, u32[]{:S(2)}) %collective-permute-start.11) | collective-permute-done | bytes 278560 | tf_op jit(solution)/shard_map/ppermute | solution.py:31
  80.1 0.6 collective-permute-start.12
  80.7 2.7 %collective-permute-start.13 = (f32[128,512]{1,0:T(8,128)S(1)}, f32[128,512]{1,0:T(8,128)S(1)}, u32[]{:S(2)}, u32[]{:S(2)}) collective-permute-start(f32[128,512]{1,0:T(8,128)S(1)} %update.1.refs_3_.old), channel_id=1, source_target_pairs={{0,64},{16,80},{32,96},{48,112},{64,0},{80,16},{96,32},{112,48},{1... | collective-permute-start | bytes 786440 | tf_op jit(solution)/shard_map/ppermute | solution.py:31
  83.4 1.5 collective-permute-start.14
  84.9 11.7 %collective-permute-done.4.refs_2_.refs_3_ = f32[768,256]{1,0:T(8,128)S(1)} collective-permute-done((f32[768,256]{1,0:T(8,128)S(1)}, f32[768,256]{1,0:T(8,128)S(1)}, u32[]{:S(2)}, u32[]{:S(2)}) %collective-permute-start.4) | collective-permute-done | bytes 786464 | tf_op jit(solution)/shard_map/ppermute | solution.py:683
  96.8 3.0 %collective-permute-start.16 = (f32[128,512]{1,0:T(8,128)S(1)}, f32[128,512]{1,0:T(8,128)S(1)}, u32[]{:S(2)}, u32[]{:S(2)}) collective-permute-start(f32[128,512]{1,0:T(8,128)S(1)} %update.1.refs_3_.old), channel_id=1, source_target_pairs={{0,128},{16,144},{32,160},{48,176},{64,192},{80,208},{96,224},{112... | collective-permute-start | bytes 786440 | tf_op jit(solution)/shard_map/ppermute | solution.py:31
  99.8 1.5 far_points.1
  101.3 4.3 %own_logits.1 = (f32[768,512]{1,0:T(8,128)S(1)}, f32[2,768]{1,0:T(2,128)S(1)}, bf16[1024,512]{1,0:T(8,128)(2,1)S(1)}, bf16[1024,512]{1,0:T(8,128)(2,1)S(1)}, f32[8,512]{1,0:T(8,128)S(1)}) custom-call(s32[1]{0:T(128)} %bitcast.me_ref.at_ref, f32[512,512]{1,0:T(8,128)S(1)} %column.2.mine_ref, f32[512,512]{1,0:T(8,128)S(1)} %collective-permute-done.15.other_ref, ...), custom_call_target="tpu_custom_call" | custom-call | flops 241591904 | bytes 681574 | tf_op jit(solution)/shard_map/own_logits/pallas_call | solution.py:320
  105.6 3.8 %far_logits.1 = (f32[768,512]{1,0:T(8,128)S(1)}, f32[2,1536]{1,0:T(2,128)S(1)}) custom-call(s32[1]{0:T(128)} %bitcast.me_ref.at_ref, bf16[1024,512]{1,0:T(8,128)(2,1)S(1)} %get-tuple-element.71.ch, bf16[1024,512]{1,0:T(8,128)(2,1)S(1)} %get-tuple-element.72.cl, f32[8,512]{1,0:T(8,128)S(1)} %get-tuple-element.73.norm, ...), custom_call_target="tpu_custom_call" | custom-call | flops 241591904 | bytes 681574 | tf_op jit(solution)/shard_map/far_logits/pallas_call | solution.py:359
  109.4 3.1 %collective-permute-start.17 = (f32[2,1536]{1,0:T(2,128)S(1)}, f32[2,1536]{1,0:T(2,128)S(1)}, u32[]{:S(2)}, u32[]{:S(2)}) collective-permute-start(f32[2,1536]{1,0:T(2,128)S(1)} %get-tuple-element.77.mine_ref.own.own_ref), channel_id=1, source_target_pairs={{0,128},{16,144},{32,160},{48,176},{64,192},{80,208},{96,224},{112... | collective-permute-start | bytes 36872 | tf_op jit(solution)/shard_map/ppermute | solution.py:31
  112.5 5.2 %collective-permute-done.17.other_ref = f32[2,1536]{1,0:T(2,128)S(1)} collective-permute-done((f32[2,1536]{1,0:T(2,128)S(1)}, f32[2,1536]{1,0:T(2,128)S(1)}, u32[]{:S(2)}, u32[]{:S(2)}) %collective-permute-start.17) | collective-permute-done | bytes 12320 | tf_op jit(solution)/shard_map/ppermute | solution.py:31
  117.7 16.9 %all_to_all.11.pin_ref.everyone.all_ref = f32[16,2,1536]{2,1,0:T(2,128)S(1)} all-to-all(f32[16,2,1536]{2,1,0:T(2,128)S(1)} %merge.1), channel_id=1, replica_groups=mesh['pts'=16,'cen'=16] {'cen'}, dimensions={0} | all-to-all | bytes 393216 | tf_op jit(solution)/shard_map/all_to_all | solution.py:712
  134.6 2.9 %collective-permute-start.19 = (f32[128,512]{1,0:T(8,128)S(1)}, f32[128,512]{1,0:T(8,128)S(1)}, u32[]{:S(2)}, u32[]{:S(2)}) collective-permute-start(f32[128,512]{1,0:T(8,128)S(1)} %relay.3.refs_1_), channel_id=1, source_target_pairs={{0,64},{16,80},{32,96},{48,112},{64,0},{80,16},{96,32},{112,48},{1... | collective-permute-start | bytes 786440 | tf_op jit(solution)/shard_map/ppermute | solution.py:31
  137.5 1.8 collective-permute-start.20
  139.3 2.9 %next_moments.2 = (f32[520,256]{1,0:T(8,128)S(1)}, f32[520,256]{1,0:T(8,128)S(1)}) custom-call(s32[1]{0:T(128)} %bitcast.me_ref.at_ref, f32[16,2,1536]{2,1,0:T(2,128)S(1)} %all_to_all.11.pin_ref.everyone.all_ref, f32[2,1536]{1,0:T(2,128)S(1)} %get-tuple-element.77.mine_ref.own.own_ref, f32[16,2,1536]{2,1,0:T(2,128)S(1)} %all_to_all.11.pin_ref.everyone.all_ref, ...), custom_call_target="tpu_custom_call" | custom-call | flops 241591904 | bytes 891289 | tf_op jit(solution)/shard_map/next_moments/pallas_call | solution.py:469
  142.4 3.0 %next_moments.3 = (f32[520,256]{1,0:T(8,128)S(1)}, f32[520,256]{1,0:T(8,128)S(1)}) custom-call(s32[1]{0:T(128)} %bitcast.me_ref.at_ref, f32[520,256]{1,0:T(8,128)S(1)} %get-tuple-element.82.pin_ref, f32[2,1536]{1,0:T(2,128)S(1)} %get-tuple-element.77.mine_ref.own.own_ref, f32[16,2,1536]{2,1,0:T(2,128)S(1)} %all_to_all.11.pin_ref.everyone.all_ref, ...), custom_call_target="tpu_custom_call" | custom-call | flops 241591904 | bytes 891289 | tf_op jit(solution)/shard_map/next_moments/pallas_call | solution.py:469
  145.9 1.2 collective-permute-done.19.refs_3_
  147.1 2.6 %collective-permute-done.20.refs_4_ = f32[128,512]{1,0:T(8,128)S(1)} collective-permute-done((f32[128,512]{1,0:T(8,128)S(1)}, f32[128,512]{1,0:T(8,128)S(1)}, u32[]{:S(2)}, u32[]{:S(2)}) %collective-permute-start.20) | collective-permute-done | bytes 262176 | tf_op jit(solution)/shard_map/ppermute | solution.py:31
  150.1 1.9 %collective-permute-start.25 = (f32[264,256]{1,0:T(8,128)S(1)}, f32[264,256]{1,0:T(8,128)S(1)}, u32[]{:S(2)}, u32[]{:S(2)}) collective-permute-start(f32[264,256]{1,0:T(8,128)S(1)} %get-tuple-element.91), channel_id=1, source_target_pairs={{0,96},{16,112},{32,64},{48,80},{64,32},{80,48},{96,0},{112,16},{1... | collective-permute-start | bytes 811016 | tf_op jit(solution)/shard_map/ppermute | solution.py:31
  152.0 7.0 %collective-permute-done.24.refs_1_ = f32[264,256]{1,0:T(8,128)S(1)} collective-permute-done((f32[264,256]{1,0:T(8,128)S(1)}, f32[264,256]{1,0:T(8,128)S(1)}, u32[]{:S(2)}, u32[]{:S(2)}) %collective-permute-start.24) | collective-permute-done | bytes 270368 | tf_op jit(solution)/shard_map/ppermute | solution.py:31
  159.0 1.3 collective-permute-done.25.refs_3_
  160.4 1.9 %collective-permute-start.26 = (f32[136,256]{1,0:T(8,128)S(1)}, f32[136,256]{1,0:T(8,128)S(1)}, u32[]{:S(2)}, u32[]{:S(2)}) collective-permute-start(f32[136,256]{1,0:T(8,128)S(1)} %get-tuple-element.93), channel_id=1, source_target_pairs={{0,96},{16,112},{32,64},{48,80},{64,32},{80,48},{96,0},{112,16},{1... | collective-permute-start | bytes 417800 | tf_op jit(solution)/shard_map/ppermute | solution.py:31
  162.2 4.7 %collective-permute-done.26.refs_1_ = f32[136,256]{1,0:T(8,128)S(1)} collective-permute-done((f32[136,256]{1,0:T(8,128)S(1)}, f32[136,256]{1,0:T(8,128)S(1)}, u32[]{:S(2)}, u32[]{:S(2)}) %collective-permute-start.26) | collective-permute-done | bytes 139296 | tf_op jit(solution)/shard_map/ppermute | solution.py:31
  167.4 1.3 collective-permute-start.28
  168.7 4.7 %weights.1 = (f32[768,1024]{1,0:T(8,128)}, f32[8,128]{1,0:T(8,128)S(1)}) custom-call(s32[1]{0:T(128)} %bitcast.me_ref.at_ref, f32[2,1536]{1,0:T(2,128)S(1)} %get-tuple-element.77.mine_ref.own.own_ref, f32[16,2,1536]{2,1,0:T(2,128)S(1)} %all_to_all.11.pin_ref.everyone.all_ref, f32[768,512]{1,0:T(8,128)S(1)} %get-tuple-element.78.e0.e_ref, ...), custom_call_target="tpu_custom_call" | custom-call | flops 241591904 | bytes 996147 | tf_op jit(solution)/shard_map/weights/pallas_call | solution.py:644
  173.4 4.0 %collective-permute-done.28.other_ref = f32[64,512]{1,0:T(8,128)S(1)} collective-permute-done((f32[64,512]{1,0:T(8,128)S(1)}, f32[64,512]{1,0:T(8,128)S(1)}, u32[]{:S(2)}, u32[]{:S(2)}) %collective-permute-start.28) | collective-permute-done | bytes 131104 | tf_op jit(solution)/shard_map/ppermute | solution.py:31
  177.4 0.7 place.1
  (39 shorter events, 3.3 us)
Async XLA Ops:
  2.3 29.4 %collective-permute-start = (f32[768,128]{1,0:T(8,128)S(1)}, f32[768,128]{1,0:T(8,128)S(1)}, u32[]{:S(2)}, u32[]{:S(2)}) collective-permute-start(f32[768,128]{1,0:T(8,128)S(1)} %own_piece.1.pin_ref), channel_id=1, source_target_pairs={{0,128},{16,144},{32,160},{48,176},{64,192},{80,208},{96,224},{112... | collective-permute-start | bytes 1179656 | tf_op jit(solution)/shard_map/ppermute | solution.py:31
  34.6 3.9 %collective-permute-start.5 = (f32[520,512]{1,0:T(8,128)S(1)}, f32[520,512]{1,0:T(8,128)S(1)}, u32[]{:S(2)}, u32[]{:S(2)}) collective-permute-start(f32[520,512]{1,0:T(8,128)S(1)} %get-tuple-element.55.pin_ref), channel_id=1, source_target_pairs={{0,16},{16,0},{32,48},{48,32},{64,80},{80,64},{96,112},{112,96},{1... | collective-permute-start | bytes 3194888 | tf_op jit(solution)/shard_map/ppermute | solution.py:31
  37.5 2.9 %collective-permute-start.6 = (f32[520,512]{1,0:T(8,128)S(1)}, f32[520,512]{1,0:T(8,128)S(1)}, u32[]{:S(2)}, u32[]{:S(2)}) collective-permute-start(f32[520,512]{1,0:T(8,128)S(1)} %get-tuple-element.56.pin_ref), channel_id=1, source_target_pairs={{0,16},{16,0},{32,48},{48,32},{64,80},{80,64},{96,112},{112,96},{1... | collective-permute-start | bytes 3194888 | tf_op jit(solution)/shard_map/ppermute | solution.py:31
  38.1 11.1 %collective-permute-start.1 = (f32[768,128]{1,0:T(8,128)S(1)}, f32[768,128]{1,0:T(8,128)S(1)}, u32[]{:S(2)}, u32[]{:S(2)}) collective-permute-start(f32[768,128]{1,0:T(8,128)S(1)} %relay.2), channel_id=1, source_target_pairs={{0,1},{1,0},{2,3},{3,2},{4,5},{5,4},{6,7},{7,6},{8,9},{9,8},{10,11... | collective-permute-start | bytes 1179656 | tf_op jit(solution)/shard_map/ppermute | solution.py:700
  40.6 14.8 %collective-permute-start.7 = (f32[264,512]{1,0:T(8,128)S(1)}, f32[264,512]{1,0:T(8,128)S(1)}, u32[]{:S(2)}, u32[]{:S(2)}) collective-permute-start(f32[264,512]{1,0:T(8,128)S(1)} %get-tuple-element.60), channel_id=1, source_target_pairs={{0,32},{16,48},{32,0},{48,16},{64,96},{80,112},{96,64},{112,80},{1... | collective-permute-start | bytes 1622024 | tf_op jit(solution)/shard_map/ppermute | solution.py:31
  42.4 15.5 %collective-permute-start.8 = (f32[264,512]{1,0:T(8,128)S(1)}, f32[264,512]{1,0:T(8,128)S(1)}, u32[]{:S(2)}, u32[]{:S(2)}) collective-permute-start(f32[264,512]{1,0:T(8,128)S(1)} %get-tuple-element.62), channel_id=1, source_target_pairs={{0,96},{16,112},{32,64},{48,80},{64,32},{80,48},{96,0},{112,16},{1... | collective-permute-start | bytes 1622024 | tf_op jit(solution)/shard_map/ppermute | solution.py:31
  49.9 33.6 %collective-permute-start.2 = (f32[768,256]{1,0:T(8,128)S(1)}, f32[768,256]{1,0:T(8,128)S(1)}, u32[]{:S(2)}, u32[]{:S(2)}) collective-permute-start(f32[768,256]{1,0:T(8,128)S(1)} %couple.1.refs_0_), channel_id=1, source_target_pairs={{0,4},{1,5},{2,6},{3,7},{4,8},{5,9},{6,10},{7,11},{8,12},{9,13},{1... | collective-permute-start | bytes 2359304 | tf_op jit(solution)/shard_map/ppermute | solution.py:683
  58.0 9.1 %collective-permute-start.9 = (f32[136,512]{1,0:T(8,128)S(1)}, f32[136,512]{1,0:T(8,128)S(1)}, u32[]{:S(2)}, u32[]{:S(2)}) collective-permute-start(f32[136,512]{1,0:T(8,128)S(1)} %get-tuple-element.64), channel_id=1, source_target_pairs={{0,96},{16,112},{32,64},{48,80},{64,32},{80,48},{96,0},{112,16},{1... | collective-permute-start | bytes 835592 | tf_op jit(solution)/shard_map/ppermute | solution.py:31
  60.2 7.5 %collective-permute-start.10 = (f32[136,512]{1,0:T(8,128)S(1)}, f32[136,512]{1,0:T(8,128)S(1)}, u32[]{:S(2)}, u32[]{:S(2)}) collective-permute-start(f32[136,512]{1,0:T(8,128)S(1)} %get-tuple-element.66), channel_id=1, source_target_pairs={{0,32},{16,48},{32,0},{48,16},{64,96},{80,112},{96,64},{112,80},{1... | collective-permute-start | bytes 835592 | tf_op jit(solution)/shard_map/ppermute | solution.py:31
  60.2 24.7 %collective-permute-start.3 = (f32[768,256]{1,0:T(8,128)S(1)}, f32[768,256]{1,0:T(8,128)S(1)}, u32[]{:S(2)}, u32[]{:S(2)}) collective-permute-start(f32[768,256]{1,0:T(8,128)S(1)} %couple.1.refs_0_), channel_id=1, source_target_pairs={{0,8},{1,9},{2,10},{3,11},{4,12},{5,13},{6,14},{7,15},{8,0},{9,1},... | collective-permute-start | bytes 2359304 | tf_op jit(solution)/shard_map/ppermute | solution.py:683
  61.6 35.0 %collective-permute-start.4 = (f32[768,256]{1,0:T(8,128)S(1)}, f32[768,256]{1,0:T(8,128)S(1)}, u32[]{:S(2)}, u32[]{:S(2)}) collective-permute-start(f32[768,256]{1,0:T(8,128)S(1)} %couple.1.refs_0_), channel_id=1, source_target_pairs={{0,12},{1,13},{2,14},{3,15},{4,0},{5,1},{6,2},{7,3},{8,4},{9,5},{1... | collective-permute-start | bytes 2359304 | tf_op jit(solution)/shard_map/ppermute | solution.py:683
  67.8 12.3 %collective-permute-start.11 = (f32[136,512]{1,0:T(8,128)S(1)}, f32[136,512]{1,0:T(8,128)S(1)}, u32[]{:S(2)}, u32[]{:S(2)}) collective-permute-start(f32[136,512]{1,0:T(8,128)S(1)} %get-tuple-element.68), channel_id=1, source_target_pairs={{0,128},{16,144},{32,160},{48,176},{64,192},{80,208},{96,224},{112... | collective-permute-start | bytes 835592 | tf_op jit(solution)/shard_map/ppermute | solution.py:31
  80.1 16.5 %collective-permute-start.12 = (f32[128,512]{1,0:T(8,128)S(1)}, f32[128,512]{1,0:T(8,128)S(1)}, u32[]{:S(2)}, u32[]{:S(2)}) collective-permute-start(f32[128,512]{1,0:T(8,128)S(1)} %update.1.refs_3_.old), channel_id=1, source_target_pairs={{0,32},{16,48},{32,0},{48,16},{64,96},{80,112},{96,64},{112,80},{1... | collective-permute-start | bytes 786440 | tf_op jit(solution)/shard_map/ppermute | solution.py:31
  80.7 15.9 %collective-permute-start.13 = (f32[128,512]{1,0:T(8,128)S(1)}, f32[128,512]{1,0:T(8,128)S(1)}, u32[]{:S(2)}, u32[]{:S(2)}) collective-permute-start(f32[128,512]{1,0:T(8,128)S(1)} %update.1.refs_3_.old), channel_id=1, source_target_pairs={{0,64},{16,80},{32,96},{48,112},{64,0},{80,16},{96,32},{112,48},{1... | collective-permute-start | bytes 786440 | tf_op jit(solution)/shard_map/ppermute | solution.py:31
  83.4 13.2 %collective-permute-start.14 = (f32[128,512]{1,0:T(8,128)S(1)}, f32[128,512]{1,0:T(8,128)S(1)}, u32[]{:S(2)}, u32[]{:S(2)}) collective-permute-start(f32[128,512]{1,0:T(8,128)S(1)} %update.1.refs_3_.old), channel_id=1, source_target_pairs={{0,96},{16,112},{32,64},{48,80},{64,32},{80,48},{96,0},{112,16},{1... | collective-permute-start | bytes 786440 | tf_op jit(solution)/shard_map/ppermute | solution.py:31
  96.7 4.6 %collective-permute-start.15 = (f32[512,512]{1,0:T(8,128)S(1)}, f32[512,512]{1,0:T(8,128)S(1)}, u32[]{:S(2)}, u32[]{:S(2)}) collective-permute-start(f32[512,512]{1,0:T(8,128)S(1)} %column.2.mine_ref), channel_id=1, source_target_pairs={{0,16},{16,0},{32,48},{48,32},{64,80},{80,64},{96,112},{112,96},{1... | collective-permute-start | bytes 3145736 | tf_op jit(solution)/shard_map/ppermute | solution.py:31
  96.8 15.7 %collective-permute-start.16 = (f32[128,512]{1,0:T(8,128)S(1)}, f32[128,512]{1,0:T(8,128)S(1)}, u32[]{:S(2)}, u32[]{:S(2)}) collective-permute-start(f32[128,512]{1,0:T(8,128)S(1)} %update.1.refs_3_.old), channel_id=1, source_target_pairs={{0,128},{16,144},{32,160},{48,176},{64,192},{80,208},{96,224},{112... | collective-permute-start | bytes 786440 | tf_op jit(solution)/shard_map/ppermute | solution.py:31
  109.4 8.2 %collective-permute-start.17 = (f32[2,1536]{1,0:T(2,128)S(1)}, f32[2,1536]{1,0:T(2,128)S(1)}, u32[]{:S(2)}, u32[]{:S(2)}) collective-permute-start(f32[2,1536]{1,0:T(2,128)S(1)} %get-tuple-element.77.mine_ref.own.own_ref), channel_id=1, source_target_pairs={{0,128},{16,144},{32,160},{48,176},{64,192},{80,208},{96,224},{112... | collective-permute-start | bytes 36872 | tf_op jit(solution)/shard_map/ppermute | solution.py:31
  134.6 11.3 %collective-permute-start.18 = (f32[128,512]{1,0:T(8,128)S(1)}, f32[128,512]{1,0:T(8,128)S(1)}, u32[]{:S(2)}, u32[]{:S(2)}) collective-permute-start(f32[128,512]{1,0:T(8,128)S(1)} %relay.3.refs_1_), channel_id=1, source_target_pairs={{0,32},{16,48},{32,0},{48,16},{64,96},{80,112},{96,64},{112,80},{1... | collective-permute-start | bytes 786440 | tf_op jit(solution)/shard_map/ppermute | solution.py:31
  134.6 12.4 %collective-permute-start.19 = (f32[128,512]{1,0:T(8,128)S(1)}, f32[128,512]{1,0:T(8,128)S(1)}, u32[]{:S(2)}, u32[]{:S(2)}) collective-permute-start(f32[128,512]{1,0:T(8,128)S(1)} %relay.3.refs_1_), channel_id=1, source_target_pairs={{0,64},{16,80},{32,96},{48,112},{64,0},{80,16},{96,32},{112,48},{1... | collective-permute-start | bytes 786440 | tf_op jit(solution)/shard_map/ppermute | solution.py:31
  137.5 12.1 %collective-permute-start.20 = (f32[128,512]{1,0:T(8,128)S(1)}, f32[128,512]{1,0:T(8,128)S(1)}, u32[]{:S(2)}, u32[]{:S(2)}) collective-permute-start(f32[128,512]{1,0:T(8,128)S(1)} %relay.3.refs_1_), channel_id=1, source_target_pairs={{0,96},{16,112},{32,64},{48,80},{64,32},{80,48},{96,0},{112,16},{1... | collective-permute-start | bytes 786440 | tf_op jit(solution)/shard_map/ppermute | solution.py:31
  142.3 7.6 %collective-permute-start.22 = (f32[520,256]{1,0:T(8,128)S(1)}, f32[520,256]{1,0:T(8,128)S(1)}, u32[]{:S(2)}, u32[]{:S(2)}) collective-permute-start(f32[520,256]{1,0:T(8,128)S(1)} %get-tuple-element.82.pin_ref), channel_id=1, source_target_pairs={{0,16},{16,0},{32,48},{48,32},{64,80},{80,64},{96,112},{112,96},{1... | collective-permute-start | bytes 1597448 | tf_op jit(solution)/shard_map/ppermute | solution.py:31
  145.3 4.5 %collective-permute-start.23 = (f32[520,256]{1,0:T(8,128)S(1)}, f32[520,256]{1,0:T(8,128)S(1)}, u32[]{:S(2)}, u32[]{:S(2)}) collective-permute-start(f32[520,256]{1,0:T(8,128)S(1)} %get-tuple-element.83.refs_0_), channel_id=1, source_target_pairs={{0,16},{16,0},{32,48},{48,32},{64,80},{80,64},{96,112},{112,96},{1... | collective-permute-start | bytes 1597448 | tf_op jit(solution)/shard_map/ppermute | solution.py:31
  149.8 18.9 %collective-permute-start.21 = (f32[512,512]{1,0:T(8,128)S(1)}, f32[512,512]{1,0:T(8,128)S(1)}, u32[]{:S(2)}, u32[]{:S(2)}) collective-permute-start(f32[512,512]{1,0:T(8,128)S(1)} %column.3.mine_ref), channel_id=1, source_target_pairs={{0,16},{16,0},{32,48},{48,32},{64,80},{80,64},{96,112},{112,96},{1... | collective-permute-start | bytes 3145736 | tf_op jit(solution)/shard_map/ppermute | solution.py:31
  150.0 9.0 %collective-permute-start.24 = (f32[264,256]{1,0:T(8,128)S(1)}, f32[264,256]{1,0:T(8,128)S(1)}, u32[]{:S(2)}, u32[]{:S(2)}) collective-permute-start(f32[264,256]{1,0:T(8,128)S(1)} %get-tuple-element.89), channel_id=1, source_target_pairs={{0,32},{16,48},{32,0},{48,16},{64,96},{80,112},{96,64},{112,80},{1... | collective-permute-start | bytes 811016 | tf_op jit(solution)/shard_map/ppermute | solution.py:31
  150.1 10.2 %collective-permute-start.25 = (f32[264,256]{1,0:T(8,128)S(1)}, f32[264,256]{1,0:T(8,128)S(1)}, u32[]{:S(2)}, u32[]{:S(2)}) collective-permute-start(f32[264,256]{1,0:T(8,128)S(1)} %get-tuple-element.91), channel_id=1, source_target_pairs={{0,96},{16,112},{32,64},{48,80},{64,32},{80,48},{96,0},{112,16},{1... | collective-permute-start | bytes 811016 | tf_op jit(solution)/shard_map/ppermute | solution.py:31
  160.4 6.6 %collective-permute-start.26 = (f32[136,256]{1,0:T(8,128)S(1)}, f32[136,256]{1,0:T(8,128)S(1)}, u32[]{:S(2)}, u32[]{:S(2)}) collective-permute-start(f32[136,256]{1,0:T(8,128)S(1)} %get-tuple-element.93), channel_id=1, source_target_pairs={{0,96},{16,112},{32,64},{48,80},{64,32},{80,48},{96,0},{112,16},{1... | collective-permute-start | bytes 417800 | tf_op jit(solution)/shard_map/ppermute | solution.py:31
  162.2 5.1 %collective-permute-start.27 = (f32[136,256]{1,0:T(8,128)S(1)}, f32[136,256]{1,0:T(8,128)S(1)}, u32[]{:S(2)}, u32[]{:S(2)}) collective-permute-start(f32[136,256]{1,0:T(8,128)S(1)} %get-tuple-element.95), channel_id=1, source_target_pairs={{0,32},{16,48},{32,0},{48,16},{64,96},{80,112},{96,64},{112,80},{1... | collective-permute-start | bytes 417800 | tf_op jit(solution)/shard_map/ppermute | solution.py:31
  167.4 10.1 %collective-permute-start.28 = (f32[64,512]{1,0:T(8,128)S(1)}, f32[64,512]{1,0:T(8,128)S(1)}, u32[]{:S(2)}, u32[]{:S(2)}) collective-permute-start(f32[64,512]{1,0:T(8,128)S(1)} %get-tuple-element.97), channel_id=1, source_target_pairs={{0,128},{16,144},{32,160},{48,176},{64,192},{80,208},{96,224},{112... | collective-permute-start | bytes 393224 | tf_op jit(solution)/shard_map/ppermute | solution.py:31
where the time goes:
time: 179 us; the launch traced here: 178 us
  waiting for transfers between devices  65 us (36%)
  starting transfers between devices  42.4 us (24%)
  Pallas kernels  39.9 us (22%)
  blocking collectives  29.9 us (17%)
    ppermute x25, waiting for transfers between devices, swap(): lax.ppermute(v, 'pts', [(i, i ^ g) for i in range(lax.axis_size('pts'))])  49.5 us
    ppermute x25, starting transfers between devices, swap(): lax.ppermute(v, 'pts', [(i, i ^ g) for i in range(lax.axis_size('pts'))])  38.6 us
    all_to_all x1, blocking collectives, local(): lax.all_to_all(merge(joint, stats, swap(stats, ZG), cen), 'cen', 0, 0)  16.9 us
    all_to_all x1, blocking collectives, local(): everyone = lax.all_to_all(copies, 'cen', 0, 0)  13 us
    ppermute x3, waiting for transfers between devices, local(): lax.ppermute(v, 'cen', [(j, (j + 4 * shift) % cen) for j in range(cen)])  11.7 us
    pallas_call x1, Pallas kernels, first_step(): pl.pallas_call(first_kernel, in_specs=[SMALL, SMALL, ANY, ANY, ANY], out_...  9.18 us
    pallas_call x2, Pallas kernels, next_moments(): pl.pallas_call(functools.partial(next_moment_kernel, order, color), in_sp...  5.89 us
    pallas_call x2, Pallas kernels, first_moments(): pl.pallas_call(functools.partial(first_moment_kernel, order, color), in_s...  5.64 us
  transfers between devices with their start and end apart: 29, of which 16 were waited for; matrix products, arithmetic and copies ran while one was open for 0% of the time, Pallas kernels for 19%

commit v1 on v0

--- a/solution.py
+++ b/solution.py
@@ -368,23 +368,23 @@
     )(me, ch, cl, norm, own, *far)
 
 
-def merge_kernel(pin_ref, mine_ref, other_ref, out_ref):
+def merge_kernel(p1, p2, p3, mine_ref, other_ref, out_ref):
     top = jnp.maximum(mine_ref[0:1, :], other_ref[0:1, :])
     total = sum(ref[1:2, :] * jnp.exp(ref[0:1, :] - top) for ref in (mine_ref, other_ref))
     for i, v in enumerate((top, total)):
         out_ref[:, i : i + 1, :] = jnp.broadcast_to(v[None], (out_ref.shape[0], *v.shape))
 
 
-def merge(pin, mine, other, copies):
+def merge(pins, mine, other, copies):
     return pl.pallas_call(
         merge_kernel,
-        in_specs=[ANY, NEAR, NEAR],
+        in_specs=[ANY] * 3 + [NEAR, NEAR],
         out_specs=NEAR,
         out_shape=jax.ShapeDtypeStruct((copies, *mine.shape), F32),
         compiler_params=params(4),
         cost_estimate=cost(copies * mine.size, 8 * copies * mine.size),
         name="merge",
-    )(pin, mine, other)
+    )(*pins, mine, other)
 
 
 def row_scale(own, everyone):
@@ -705,13 +705,12 @@
     keep, send = part(swapped(units, 2))
     share = update(keep, swap(send, ZG), old)
     joint = swap(share, ZG)
-    mine = column([share] + [swap(share, mask) for mask in X_PEERS], *quarters[1:])
+    mine = column([share] + [swap(share, mask) for mask in X_PEERS], *quarters[1:], joint)
     fh, fl, gh, gl = far_points(at, quarters)
     e_own, stats, ch, cl, norm = own_logits(me, mine, swap(mine, CORE), (xh, xl))
+    peers = [joint] + [swap(joint, mask) for mask in X_PEERS]
     e_far, stats = far_logits(me, ch, cl, norm, stats, (fh, fl))
-    everyone = lax.all_to_all(merge(joint, stats, swap(stats, ZG), cen), "cen", 0, 0)
-    joint = relay(joint, everyone)
-    peers = [joint] + [swap(joint, mask) for mask in X_PEERS]
+    everyone = lax.all_to_all(merge(peers[1:], stats, swap(stats, ZG), cen), "cen", 0, 0)
     units, pin = [], everyone
     for u, order in enumerate(orders):
         units.append(

time: 179 us -> 176 us (0.983)
  waiting for transfers between devices: 65 us -> 61.1 us
    ppermute x3, waiting for transfers between devices: 11.7 us -> 0.01 us  [local(): lax.ppermute(v, 'cen', [(j, (j + 4 * shift) % cen) for j in range(cen)])]
    ppermute x25, waiting for transfers between devices: 49.5 us -> 57.4 us  [swap(): lax.ppermute(v, 'pts', [(i, i ^ g) for i in range(lax.axis_size('pts'))])]
  transfers between devices with their start and end apart: 29 -> 29, of which waited for: 16 -> 19; matrix products, arithmetic and copies ran while one was open for 0% -> 0% of each run, Pallas kernels for 19% -> 18%
where the time goes in v1:
time: 176 us; the launch traced here: 175 us
  waiting for transfers between devices  61.1 us (35%)
  starting transfers between devices  42.6 us (24%)
  Pallas kernels  39.9 us (23%)
  blocking collectives  30.6 us (17%)
    ppermute x25, waiting for transfers between devices, swap(): lax.ppermute(v, 'pts', [(i, i ^ g) for i in range(lax.axis_size('pts'))])  57.4 us
    ppermute x25, starting transfers between devices, swap(): lax.ppermute(v, 'pts', [(i, i ^ g) for i in range(lax.axis_size('pts'))])  37.3 us
    all_to_all x1, blocking collectives, local(): lax.all_to_all(merge(peers[1:], stats, swap(stats, ZG), cen), 'cen', 0, 0)  17.6 us
    all_to_all x1, blocking collectives, local(): everyone = lax.all_to_all(copies, 'cen', 0, 0)  13 us
    pallas_call x1, Pallas kernels, first_step(): pl.pallas_call(first_kernel, in_specs=[SMALL, SMALL, ANY, ANY, ANY], out_...  9.18 us
    pallas_call x2, Pallas kernels, next_moments(): pl.pallas_call(functools.partial(next_moment_kernel, order, color), in_sp...  5.89 us
    pallas_call x2, Pallas kernels, first_moments(): pl.pallas_call(functools.partial(first_moment_kernel, order, color), in_s...  5.64 us
    ppermute x3, starting transfers between devices, local(): lax.ppermute(v, 'cen', [(j, (j + 4 * shift) % cen) for j in range(cen)])  5.06 us
  transfers between devices with their start and end apart: 29, of which 19 were waited for; matrix products, arithmetic and copies ran while one was open for 0% of the time, Pallas kernels for 18%

profile of v1, /device:TPU:8, one launch (start us, length us, event | category | flops | bytes accessed | tf_op | source)
XLA Modules:
  0.0 175.1 jit_solution(7859847234319498058)
XLA Ops:
  0.7 1.6 own_piece.1.pin_ref
  2.3 7.3 %collective-permute-start = (f32[768,128]{1,0:T(8,128)S(1)}, f32[768,128]{1,0:T(8,128)S(1)}, u32[]{:S(2)}, u32[]{:S(2)}) collective-permute-start(f32[768,128]{1,0:T(8,128)S(1)} %own_piece.1.pin_ref), channel_id=1, source_target_pairs={{0,128},{16,144},{32,160},{48,176},{64,192},{80,208},{96,224},{112... | collective-permute-start | bytes 1179656 | tf_op jit(solution)/shard_map/ppermute | solution.py:31
  9.6 9.2 %first_logits.1 = (f32[768,1024]{1,0:T(8,128)S(1)}, f32[2,768]{1,0:T(2,128)S(1)}, f32[16,2,768]{2,1,0:T(2,128)S(1)}, bf16[768,1024]{1,0:T(8,128)(2,1)S(1)}, bf16...) custom-call(s32[1]{0:T(128)} %bitcast.me_ref.at_ref, ...), custom_call_target="tpu_custom_call" | custom-call | flops 9663676416 | bytes 1363148 | tf_op jit(solution)/shard_map/first_logits/pallas_call | solution.py:167
  18.8 13.0 %all_to_all.10.all_ref = f32[16,2,768]{2,1,0:T(2,128)S(1)} all-to-all(f32[16,2,768]{2,1,0:T(2,128)S(1)} %get-tuple-element.51), channel_id=1, replica_groups=mesh['pts'=16,'cen'=16] {'cen'}, dimensions={0} | all-to-all | bytes 196608 | tf_op jit(solution)/shard_map/all_to_all | solution.py:690
  31.8 2.8 %first_moments.2 = (f32[520,512]{1,0:T(8,128)S(1)}, f32[520,512]{1,0:T(8,128)S(1)}) custom-call(s32[1]{0:T(128)} %bitcast.me_ref.at_ref, f32[768,128]{1,0:T(8,128)S(1)} %collective-permute-done.pin_ref.mine_ref, f32[2,768]{1,0:T(2,128)S(1)} %get-tuple-element.50.own_ref, f32[16,2,768]{2,1,0:T(2,128)S(1)} %all_to_all.10.all_ref, ...), custom_call_target="tpu_custom_call" | custom-call | flops 241591904 | bytes 681574 | tf_op jit(solution)/shard_map/first_moments/pallas_call | solution.py:435
  34.7 2.8 %first_moments.3 = (f32[520,512]{1,0:T(8,128)S(1)}, f32[520,512]{1,0:T(8,128)S(1)}) custom-call(s32[1]{0:T(128)} %bitcast.me_ref.at_ref, f32[520,512]{1,0:T(8,128)S(1)} %get-tuple-element.55.pin_ref, f32[2,768]{1,0:T(2,128)S(1)} %get-tuple-element.50.own_ref, f32[16,2,768]{2,1,0:T(2,128)S(1)} %all_to_all.10.all_ref, ...), custom_call_target="tpu_custom_call" | custom-call | flops 241591904 | bytes 681574 | tf_op jit(solution)/shard_map/first_moments/pallas_call | solution.py:435
  38.5 1.9 %collective-permute-done.6.refs_3_ = f32[520,512]{1,0:T(8,128)S(1)} collective-permute-done((f32[520,512]{1,0:T(8,128)S(1)}, f32[520,512]{1,0:T(8,128)S(1)}, u32[]{:S(2)}, u32[]{:S(2)}) %collective-permute-start.6) | collective-permute-done | bytes 1064992 | tf_op jit(solution)/shard_map/ppermute | solution.py:31
  40.6 1.8 %collective-permute-start.7 = (f32[264,512]{1,0:T(8,128)S(1)}, f32[264,512]{1,0:T(8,128)S(1)}, u32[]{:S(2)}, u32[]{:S(2)}) collective-permute-start(f32[264,512]{1,0:T(8,128)S(1)} %get-tuple-element.60), channel_id=1, source_target_pairs={{0,32},{16,48},{32,0},{48,16},{64,96},{80,112},{96,64},{112,80},{1... | collective-permute-start | bytes 1622024 | tf_op jit(solution)/shard_map/ppermute | solution.py:31
  42.4 2.1 %collective-permute-start.8 = (f32[264,512]{1,0:T(8,128)S(1)}, f32[264,512]{1,0:T(8,128)S(1)}, u32[]{:S(2)}, u32[]{:S(2)}) collective-permute-start(f32[264,512]{1,0:T(8,128)S(1)} %get-tuple-element.62), channel_id=1, source_target_pairs={{0,96},{16,112},{32,64},{48,80},{64,32},{80,48},{96,0},{112,16},{1... | collective-permute-start | bytes 1622024 | tf_op jit(solution)/shard_map/ppermute | solution.py:31
  44.5 1.0 old_block.1.pin_ref.refs_2_
  45.5 3.8 %collective-permute-done.1.other_ref = f32[768,128]{1,0:T(8,128)S(1)} collective-permute-done((f32[768,128]{1,0:T(8,128)S(1)}, f32[768,128]{1,0:T(8,128)S(1)}, u32[]{:S(2)}, u32[]{:S(2)}) %collective-permute-start.1) | collective-permute-done | bytes 393248 | tf_op jit(solution)/shard_map/ppermute | solution.py:700
  49.9 0.8 collective-permute-start.2
  50.6 2.8 %collective-permute-start.3 = (f32[768,256]{1,0:T(8,128)S(1)}, f32[768,256]{1,0:T(8,128)S(1)}, u32[]{:S(2)}, u32[]{:S(2)}) collective-permute-start(f32[768,256]{1,0:T(8,128)S(1)} %couple.1.refs_0_), channel_id=1, source_target_pairs={{0,8},{1,9},{2,10},{3,11},{4,12},{5,13},{6,14},{7,15},{8,0},{9,1},... | collective-permute-start | bytes 2359304 | tf_op jit(solution)/shard_map/ppermute | solution.py:683
  53.5 2.0 %collective-permute-done.7.refs_2_ = f32[264,512]{1,0:T(8,128)S(1)} collective-permute-done((f32[264,512]{1,0:T(8,128)S(1)}, f32[264,512]{1,0:T(8,128)S(1)}, u32[]{:S(2)}, u32[]{:S(2)}) %collective-permute-start.7) | collective-permute-done | bytes 540704 | tf_op jit(solution)/shard_map/ppermute | solution.py:31
  55.4 2.4 %collective-permute-done.8.refs_4_ = f32[264,512]{1,0:T(8,128)S(1)} collective-permute-done((f32[264,512]{1,0:T(8,128)S(1)}, f32[264,512]{1,0:T(8,128)S(1)}, u32[]{:S(2)}, u32[]{:S(2)}) %collective-permute-start.8) | collective-permute-done | bytes 540704 | tf_op jit(solution)/shard_map/ppermute | solution.py:31
  58.0 2.2 %collective-permute-start.9 = (f32[136,512]{1,0:T(8,128)S(1)}, f32[136,512]{1,0:T(8,128)S(1)}, u32[]{:S(2)}, u32[]{:S(2)}) collective-permute-start(f32[136,512]{1,0:T(8,128)S(1)} %get-tuple-element.64), channel_id=1, source_target_pairs={{0,96},{16,112},{32,64},{48,80},{64,32},{80,48},{96,0},{112,16},{1... | collective-permute-start | bytes 835592 | tf_op jit(solution)/shard_map/ppermute | solution.py:31
  60.2 1.5 collective-permute-start.4
  61.6 5.5 %collective-permute-done.9.refs_1_ = f32[136,512]{1,0:T(8,128)S(1)} collective-permute-done((f32[136,512]{1,0:T(8,128)S(1)}, f32[136,512]{1,0:T(8,128)S(1)}, u32[]{:S(2)}, u32[]{:S(2)}) %collective-permute-start.9) | collective-permute-done | bytes 278560 | tf_op jit(solution)/shard_map/ppermute | solution.py:31
  67.8 3.0 %collective-permute-start.11 = (f32[136,512]{1,0:T(8,128)S(1)}, f32[136,512]{1,0:T(8,128)S(1)}, u32[]{:S(2)}, u32[]{:S(2)}) collective-permute-start(f32[136,512]{1,0:T(8,128)S(1)} %get-tuple-element.68), channel_id=1, source_target_pairs={{0,128},{16,144},{32,160},{48,176},{64,192},{80,208},{96,224},{112... | collective-permute-start | bytes 835592 | tf_op jit(solution)/shard_map/ppermute | solution.py:31
  70.8 9.3 %collective-permute-done.11.refs_1_ = f32[136,512]{1,0:T(8,128)S(1)} collective-permute-done((f32[136,512]{1,0:T(8,128)S(1)}, f32[136,512]{1,0:T(8,128)S(1)}, u32[]{:S(2)}, u32[]{:S(2)}) %collective-permute-start.11) | collective-permute-done | bytes 278560 | tf_op jit(solution)/shard_map/ppermute | solution.py:31
  80.1 4.5 %collective-permute-start.12 = (f32[128,512]{1,0:T(8,128)S(1)}, f32[128,512]{1,0:T(8,128)S(1)}, u32[]{:S(2)}, u32[]{:S(2)}) collective-permute-start(f32[128,512]{1,0:T(8,128)S(1)} %update.1.refs_4_.old), channel_id=1, source_target_pairs={{0,128},{16,144},{32,160},{48,176},{64,192},{80,208},{96,224},{112... | collective-permute-start | bytes 786440 | tf_op jit(solution)/shard_map/ppermute | solution.py:31
  85.2 2.7 %collective-permute-start.14 = (f32[128,512]{1,0:T(8,128)S(1)}, f32[128,512]{1,0:T(8,128)S(1)}, u32[]{:S(2)}, u32[]{:S(2)}) collective-permute-start(f32[128,512]{1,0:T(8,128)S(1)} %update.1.refs_4_.old), channel_id=1, source_target_pairs={{0,64},{16,80},{32,96},{48,112},{64,0},{80,16},{96,32},{112,48},{1... | collective-permute-start | bytes 786440 | tf_op jit(solution)/shard_map/ppermute | solution.py:31
  87.8 1.5 collective-permute-start.15
  89.3 2.0 %collective-permute-done.12.refs_3_.refs_1_ = f32[128,512]{1,0:T(8,128)S(1)} collective-permute-done((f32[128,512]{1,0:T(8,128)S(1)}, f32[128,512]{1,0:T(8,128)S(1)}, u32[]{:S(2)}, u32[]{:S(2)}) %collective-permute-start.12) | collective-permute-done | bytes 262176 | tf_op jit(solution)/shard_map/ppermute | solution.py:31
  91.3 0.9 collective-permute-done.13.refs_5_
  92.2 4.4 %collective-permute-done.14.refs_6_ = f32[128,512]{1,0:T(8,128)S(1)} collective-permute-done((f32[128,512]{1,0:T(8,128)S(1)}, f32[128,512]{1,0:T(8,128)S(1)}, u32[]{:S(2)}, u32[]{:S(2)}) %collective-permute-start.14) | collective-permute-done | bytes 262176 | tf_op jit(solution)/shard_map/ppermute | solution.py:31
  96.6 2.5 %collective-permute-done.15.refs_7_ = f32[128,512]{1,0:T(8,128)S(1)} collective-permute-done((f32[128,512]{1,0:T(8,128)S(1)}, f32[128,512]{1,0:T(8,128)S(1)}, u32[]{:S(2)}, u32[]{:S(2)}) %collective-permute-start.15) | collective-permute-done | bytes 262176 | tf_op jit(solution)/shard_map/ppermute | solution.py:31
  99.4 2.6 %collective-permute-start.18 = (f32[128,512]{1,0:T(8,128)S(1)}, f32[128,512]{1,0:T(8,128)S(1)}, u32[]{:S(2)}, u32[]{:S(2)}) collective-permute-start(f32[128,512]{1,0:T(8,128)S(1)} %collective-permute-done.12.refs_3_.refs_1_), channel_id=1, source_target_pairs={{0,64},{16,80},{32,96},{48,112},{64,0},{80,16},{96,32},{112,48},{1... | collective-permute-start | bytes 786440 | tf_op jit(solution)/shard_map/ppermute | solution.py:31
  102.1 2.1 %collective-permute-start.19 = (f32[128,512]{1,0:T(8,128)S(1)}, f32[128,512]{1,0:T(8,128)S(1)}, u32[]{:S(2)}, u32[]{:S(2)}) collective-permute-start(f32[128,512]{1,0:T(8,128)S(1)} %collective-permute-done.12.refs_3_.refs_1_), channel_id=1, source_target_pairs={{0,96},{16,112},{32,64},{48,80},{64,32},{80,48},{96,0},{112,16},{1... | collective-permute-start | bytes 786440 | tf_op jit(solution)/shard_map/ppermute | solution.py:31
  104.1 1.5 far_points.1
  105.6 4.3 %own_logits.1 = (f32[768,512]{1,0:T(8,128)S(1)}, f32[2,768]{1,0:T(2,128)S(1)}, bf16[1024,512]{1,0:T(8,128)(2,1)S(1)}, bf16[1024,512]{1,0:T(8,128)(2,1)S(1)}, f32[8,512]{1,0:T(8,128)S(1)}) custom-call(s32[1]{0:T(128)} %bitcast.me_ref.at_ref, f32[512,512]{1,0:T(8,128)S(1)} %column.2.mine_ref, f32[512,512]{1,0:T(8,128)S(1)} %collective-permute-done.16.other_ref, ...), custom_call_target="tpu_custom_call" | custom-call | flops 241591904 | bytes 681574 | tf_op jit(solution)/shard_map/own_logits/pallas_call | solution.py:320
  109.9 3.8 %far_logits.1 = (f32[768,512]{1,0:T(8,128)S(1)}, f32[2,1536]{1,0:T(2,128)S(1)}) custom-call(s32[1]{0:T(128)} %bitcast.me_ref.at_ref, bf16[1024,512]{1,0:T(8,128)(2,1)S(1)} %get-tuple-element.71.ch, bf16[1024,512]{1,0:T(8,128)(2,1)S(1)} %get-tuple-element.72.cl, f32[8,512]{1,0:T(8,128)S(1)} %get-tuple-element.73.norm, ...), custom_call_target="tpu_custom_call" | custom-call | flops 241591904 | bytes 681574 | tf_op jit(solution)/shard_map/far_logits/pallas_call | solution.py:359
  113.7 0.8 collective-permute-start.20
  114.6 2.4 %collective-permute-done.19.p3.refs_4_ = f32[128,512]{1,0:T(8,128)S(1)} collective-permute-done((f32[128,512]{1,0:T(8,128)S(1)}, f32[128,512]{1,0:T(8,128)S(1)}, u32[]{:S(2)}, u32[]{:S(2)}) %collective-permute-start.19) | collective-permute-done | bytes 262176 | tf_op jit(solution)/shard_map/ppermute | solution.py:31
  117.0 4.7 %collective-permute-done.20.other_ref = f32[2,1536]{1,0:T(2,128)S(1)} collective-permute-done((f32[2,1536]{1,0:T(2,128)S(1)}, f32[2,1536]{1,0:T(2,128)S(1)}, u32[]{:S(2)}, u32[]{:S(2)}) %collective-permute-start.20) | collective-permute-done | bytes 12320 | tf_op jit(solution)/shard_map/ppermute | solution.py:31
  121.7 17.6 %all_to_all.11.pin_ref.everyone.all_ref = f32[16,2,1536]{2,1,0:T(2,128)S(1)} all-to-all(f32[16,2,1536]{2,1,0:T(2,128)S(1)} %merge.1), channel_id=1, replica_groups=mesh['pts'=16,'cen'=16] {'cen'}, dimensions={0} | all-to-all | bytes 393216 | tf_op jit(solution)/shard_map/all_to_all | solution.py:713
  139.2 2.9 %next_moments.2 = (f32[520,256]{1,0:T(8,128)S(1)}, f32[520,256]{1,0:T(8,128)S(1)}) custom-call(s32[1]{0:T(128)} %bitcast.me_ref.at_ref, f32[16,2,1536]{2,1,0:T(2,128)S(1)} %all_to_all.11.pin_ref.everyone.all_ref, f32[2,1536]{1,0:T(2,128)S(1)} %get-tuple-element.77.mine_ref.own.own_ref, f32[16,2,1536]{2,1,0:T(2,128)S(1)} %all_to_all.11.pin_ref.everyone.all_ref, ...), custom_call_target="tpu_custom_call" | custom-call | flops 241591904 | bytes 891289 | tf_op jit(solution)/shard_map/next_moments/pallas_call | solution.py:469
  142.3 3.0 %next_moments.3 = (f32[520,256]{1,0:T(8,128)S(1)}, f32[520,256]{1,0:T(8,128)S(1)}) custom-call(s32[1]{0:T(128)} %bitcast.me_ref.at_ref, f32[520,256]{1,0:T(8,128)S(1)} %get-tuple-element.82.pin_ref, f32[2,1536]{1,0:T(2,128)S(1)} %get-tuple-element.77.mine_ref.own.own_ref, f32[16,2,1536]{2,1,0:T(2,128)S(1)} %all_to_all.11.pin_ref.everyone.all_ref, ...), custom_call_target="tpu_custom_call" | custom-call | flops 241591904 | bytes 891289 | tf_op jit(solution)/shard_map/next_moments/pallas_call | solution.py:469
  146.0 1.4 collective-permute-done.23.refs_3_
  147.6 1.6 collective-permute-start.25
  149.2 7.2 %collective-permute-done.24.refs_1_ = f32[264,256]{1,0:T(8,128)S(1)} collective-permute-done((f32[264,256]{1,0:T(8,128)S(1)}, f32[264,256]{1,0:T(8,128)S(1)}, u32[]{:S(2)}, u32[]{:S(2)}) %collective-permute-start.24) | collective-permute-done | bytes 270368 | tf_op jit(solution)/shard_map/ppermute | solution.py:31
  156.4 1.3 collective-permute-done.25.refs_3_
  157.8 1.5 collective-permute-start.26
  159.3 4.9 %collective-permute-done.26.refs_1_ = f32[136,256]{1,0:T(8,128)S(1)} collective-permute-done((f32[136,256]{1,0:T(8,128)S(1)}, f32[136,256]{1,0:T(8,128)S(1)}, u32[]{:S(2)}, u32[]{:S(2)}) %collective-permute-start.26) | collective-permute-done | bytes 139296 | tf_op jit(solution)/shard_map/ppermute | solution.py:31
  164.4 1.4 collective-permute-start.28
  165.8 4.7 %weights.1 = (f32[768,1024]{1,0:T(8,128)}, f32[8,128]{1,0:T(8,128)S(1)}) custom-call(s32[1]{0:T(128)} %bitcast.me_ref.at_ref, f32[2,1536]{1,0:T(2,128)S(1)} %get-tuple-element.77.mine_ref.own.own_ref, f32[16,2,1536]{2,1,0:T(2,128)S(1)} %all_to_all.11.pin_ref.everyone.all_ref, f32[768,512]{1,0:T(8,128)S(1)} %get-tuple-element.78.e0.e_ref, ...), custom_call_target="tpu_custom_call" | custom-call | flops 241591904 | bytes 996147 | tf_op jit(solution)/shard_map/weights/pallas_call | solution.py:644
  170.5 3.9 %collective-permute-done.28.other_ref = f32[64,512]{1,0:T(8,128)S(1)} collective-permute-done((f32[64,512]{1,0:T(8,128)S(1)}, f32[64,512]{1,0:T(8,128)S(1)}, u32[]{:S(2)}, u32[]{:S(2)}) %collective-permute-start.28) | collective-permute-done | bytes 131104 | tf_op jit(solution)/shard_map/ppermute | solution.py:31
  174.4 0.7 place.1
  (38 shorter events, 5.0 us)
Async XLA Ops:
  2.3 29.4 %collective-permute-start = (f32[768,128]{1,0:T(8,128)S(1)}, f32[768,128]{1,0:T(8,128)S(1)}, u32[]{:S(2)}, u32[]{:S(2)}) collective-permute-start(f32[768,128]{1,0:T(8,128)S(1)} %own_piece.1.pin_ref), channel_id=1, source_target_pairs={{0,128},{16,144},{32,160},{48,176},{64,192},{80,208},{96,224},{112... | collective-permute-start | bytes 1179656 | tf_op jit(solution)/shard_map/ppermute | solution.py:31
  34.6 3.9 %collective-permute-start.5 = (f32[520,512]{1,0:T(8,128)S(1)}, f32[520,512]{1,0:T(8,128)S(1)}, u32[]{:S(2)}, u32[]{:S(2)}) collective-permute-start(f32[520,512]{1,0:T(8,128)S(1)} %get-tuple-element.55.pin_ref), channel_id=1, source_target_pairs={{0,16},{16,0},{32,48},{48,32},{64,80},{80,64},{96,112},{112,96},{1... | collective-permute-start | bytes 3194888 | tf_op jit(solution)/shard_map/ppermute | solution.py:31
  37.5 2.9 %collective-permute-start.6 = (f32[520,512]{1,0:T(8,128)S(1)}, f32[520,512]{1,0:T(8,128)S(1)}, u32[]{:S(2)}, u32[]{:S(2)}) collective-permute-start(f32[520,512]{1,0:T(8,128)S(1)} %get-tuple-element.56.pin_ref), channel_id=1, source_target_pairs={{0,16},{16,0},{32,48},{48,32},{64,80},{80,64},{96,112},{112,96},{1... | collective-permute-start | bytes 3194888 | tf_op jit(solution)/shard_map/ppermute | solution.py:31
  38.1 11.1 %collective-permute-start.1 = (f32[768,128]{1,0:T(8,128)S(1)}, f32[768,128]{1,0:T(8,128)S(1)}, u32[]{:S(2)}, u32[]{:S(2)}) collective-permute-start(f32[768,128]{1,0:T(8,128)S(1)} %relay.1), channel_id=1, source_target_pairs={{0,1},{1,0},{2,3},{3,2},{4,5},{5,4},{6,7},{7,6},{8,9},{9,8},{10,11... | collective-permute-start | bytes 1179656 | tf_op jit(solution)/shard_map/ppermute | solution.py:700
  40.6 14.8 %collective-permute-start.7 = (f32[264,512]{1,0:T(8,128)S(1)}, f32[264,512]{1,0:T(8,128)S(1)}, u32[]{:S(2)}, u32[]{:S(2)}) collective-permute-start(f32[264,512]{1,0:T(8,128)S(1)} %get-tuple-element.60), channel_id=1, source_target_pairs={{0,32},{16,48},{32,0},{48,16},{64,96},{80,112},{96,64},{112,80},{1... | collective-permute-start | bytes 1622024 | tf_op jit(solution)/shard_map/ppermute | solution.py:31
  42.4 15.5 %collective-permute-start.8 = (f32[264,512]{1,0:T(8,128)S(1)}, f32[264,512]{1,0:T(8,128)S(1)}, u32[]{:S(2)}, u32[]{:S(2)}) collective-permute-start(f32[264,512]{1,0:T(8,128)S(1)} %get-tuple-element.62), channel_id=1, source_target_pairs={{0,96},{16,112},{32,64},{48,80},{64,32},{80,48},{96,0},{112,16},{1... | collective-permute-start | bytes 1622024 | tf_op jit(solution)/shard_map/ppermute | solution.py:31
  49.9 35.3 %collective-permute-start.2 = (f32[768,256]{1,0:T(8,128)S(1)}, f32[768,256]{1,0:T(8,128)S(1)}, u32[]{:S(2)}, u32[]{:S(2)}) collective-permute-start(f32[768,256]{1,0:T(8,128)S(1)} %couple.1.refs_0_), channel_id=1, source_target_pairs={{0,4},{1,5},{2,6},{3,7},{4,8},{5,9},{6,10},{7,11},{8,12},{9,13},{1... | collective-permute-start | bytes 2359304 | tf_op jit(solution)/shard_map/ppermute | solution.py:683
  50.6 37.2 %collective-permute-start.3 = (f32[768,256]{1,0:T(8,128)S(1)}, f32[768,256]{1,0:T(8,128)S(1)}, u32[]{:S(2)}, u32[]{:S(2)}) collective-permute-start(f32[768,256]{1,0:T(8,128)S(1)} %couple.1.refs_0_), channel_id=1, source_target_pairs={{0,8},{1,9},{2,10},{3,11},{4,12},{5,13},{6,14},{7,15},{8,0},{9,1},... | collective-permute-start | bytes 2359304 | tf_op jit(solution)/shard_map/ppermute | solution.py:683
  58.0 9.1 %collective-permute-start.9 = (f32[136,512]{1,0:T(8,128)S(1)}, f32[136,512]{1,0:T(8,128)S(1)}, u32[]{:S(2)}, u32[]{:S(2)}) collective-permute-start(f32[136,512]{1,0:T(8,128)S(1)} %get-tuple-element.64), channel_id=1, source_target_pairs={{0,96},{16,112},{32,64},{48,80},{64,32},{80,48},{96,0},{112,16},{1... | collective-permute-start | bytes 835592 | tf_op jit(solution)/shard_map/ppermute | solution.py:31
  60.2 7.5 %collective-permute-start.10 = (f32[136,512]{1,0:T(8,128)S(1)}, f32[136,512]{1,0:T(8,128)S(1)}, u32[]{:S(2)}, u32[]{:S(2)}) collective-permute-start(f32[136,512]{1,0:T(8,128)S(1)} %get-tuple-element.66), channel_id=1, source_target_pairs={{0,32},{16,48},{32,0},{48,16},{64,96},{80,112},{96,64},{112,80},{1... | collective-permute-start | bytes 835592 | tf_op jit(solution)/shard_map/ppermute | solution.py:31
  60.2 29.2 %collective-permute-start.4 = (f32[768,256]{1,0:T(8,128)S(1)}, f32[768,256]{1,0:T(8,128)S(1)}, u32[]{:S(2)}, u32[]{:S(2)}) collective-permute-start(f32[768,256]{1,0:T(8,128)S(1)} %couple.1.refs_0_), channel_id=1, source_target_pairs={{0,12},{1,13},{2,14},{3,15},{4,0},{5,1},{6,2},{7,3},{8,4},{9,5},{1... | collective-permute-start | bytes 2359304 | tf_op jit(solution)/shard_map/ppermute | solution.py:683
  67.8 12.3 %collective-permute-start.11 = (f32[136,512]{1,0:T(8,128)S(1)}, f32[136,512]{1,0:T(8,128)S(1)}, u32[]{:S(2)}, u32[]{:S(2)}) collective-permute-start(f32[136,512]{1,0:T(8,128)S(1)} %get-tuple-element.68), channel_id=1, source_target_pairs={{0,128},{16,144},{32,160},{48,176},{64,192},{80,208},{96,224},{112... | collective-permute-start | bytes 835592 | tf_op jit(solution)/shard_map/ppermute | solution.py:31
  80.1 11.2 %collective-permute-start.12 = (f32[128,512]{1,0:T(8,128)S(1)}, f32[128,512]{1,0:T(8,128)S(1)}, u32[]{:S(2)}, u32[]{:S(2)}) collective-permute-start(f32[128,512]{1,0:T(8,128)S(1)} %update.1.refs_4_.old), channel_id=1, source_target_pairs={{0,128},{16,144},{32,160},{48,176},{64,192},{80,208},{96,224},{112... | collective-permute-start | bytes 786440 | tf_op jit(solution)/shard_map/ppermute | solution.py:31
  84.6 7.6 %collective-permute-start.13 = (f32[128,512]{1,0:T(8,128)S(1)}, f32[128,512]{1,0:T(8,128)S(1)}, u32[]{:S(2)}, u32[]{:S(2)}) collective-permute-start(f32[128,512]{1,0:T(8,128)S(1)} %update.1.refs_4_.old), channel_id=1, source_target_pairs={{0,32},{16,48},{32,0},{48,16},{64,96},{80,112},{96,64},{112,80},{1... | collective-permute-start | bytes 786440 | tf_op jit(solution)/shard_map/ppermute | solution.py:31
  85.2 11.5 %collective-permute-start.14 = (f32[128,512]{1,0:T(8,128)S(1)}, f32[128,512]{1,0:T(8,128)S(1)}, u32[]{:S(2)}, u32[]{:S(2)}) collective-permute-start(f32[128,512]{1,0:T(8,128)S(1)} %update.1.refs_4_.old), channel_id=1, source_target_pairs={{0,64},{16,80},{32,96},{48,112},{64,0},{80,16},{96,32},{112,48},{1... | collective-permute-start | bytes 786440 | tf_op jit(solution)/shard_map/ppermute | solution.py:31
  87.8 11.3 %collective-permute-start.15 = (f32[128,512]{1,0:T(8,128)S(1)}, f32[128,512]{1,0:T(8,128)S(1)}, u32[]{:S(2)}, u32[]{:S(2)}) collective-permute-start(f32[128,512]{1,0:T(8,128)S(1)} %update.1.refs_4_.old), channel_id=1, source_target_pairs={{0,96},{16,112},{32,64},{48,80},{64,32},{80,48},{96,0},{112,16},{1... | collective-permute-start | bytes 786440 | tf_op jit(solution)/shard_map/ppermute | solution.py:31
  99.2 6.4 %collective-permute-start.16 = (f32[512,512]{1,0:T(8,128)S(1)}, f32[512,512]{1,0:T(8,128)S(1)}, u32[]{:S(2)}, u32[]{:S(2)}) collective-permute-start(f32[512,512]{1,0:T(8,128)S(1)} %column.2.mine_ref), channel_id=1, source_target_pairs={{0,16},{16,0},{32,48},{48,32},{64,80},{80,64},{96,112},{112,96},{1... | collective-permute-start | bytes 3145736 | tf_op jit(solution)/shard_map/ppermute | solution.py:31
  99.3 15.2 %collective-permute-start.17 = (f32[128,512]{1,0:T(8,128)S(1)}, f32[128,512]{1,0:T(8,128)S(1)}, u32[]{:S(2)}, u32[]{:S(2)}) collective-permute-start(f32[128,512]{1,0:T(8,128)S(1)} %collective-permute-done.12.refs_3_.refs_1_), channel_id=1, source_target_pairs={{0,32},{16,48},{32,0},{48,16},{64,96},{80,112},{96,64},{112,80},{1... | collective-permute-start | bytes 786440 | tf_op jit(solution)/shard_map/ppermute | solution.py:31
  99.4 15.2 %collective-permute-start.18 = (f32[128,512]{1,0:T(8,128)S(1)}, f32[128,512]{1,0:T(8,128)S(1)}, u32[]{:S(2)}, u32[]{:S(2)}) collective-permute-start(f32[128,512]{1,0:T(8,128)S(1)} %collective-permute-done.12.refs_3_.refs_1_), channel_id=1, source_target_pairs={{0,64},{16,80},{32,96},{48,112},{64,0},{80,16},{96,32},{112,48},{1... | collective-permute-start | bytes 786440 | tf_op jit(solution)/shard_map/ppermute | solution.py:31
  102.1 14.9 %collective-permute-start.19 = (f32[128,512]{1,0:T(8,128)S(1)}, f32[128,512]{1,0:T(8,128)S(1)}, u32[]{:S(2)}, u32[]{:S(2)}) collective-permute-start(f32[128,512]{1,0:T(8,128)S(1)} %collective-permute-done.12.refs_3_.refs_1_), channel_id=1, source_target_pairs={{0,96},{16,112},{32,64},{48,80},{64,32},{80,48},{96,0},{112,16},{1... | collective-permute-start | bytes 786440 | tf_op jit(solution)/shard_map/ppermute | solution.py:31
  113.7 7.9 %collective-permute-start.20 = (f32[2,1536]{1,0:T(2,128)S(1)}, f32[2,1536]{1,0:T(2,128)S(1)}, u32[]{:S(2)}, u32[]{:S(2)}) collective-permute-start(f32[2,1536]{1,0:T(2,128)S(1)} %get-tuple-element.77.mine_ref.own.own_ref), channel_id=1, source_target_pairs={{0,128},{16,144},{32,160},{48,176},{64,192},{80,208},{96,224},{112... | collective-permute-start | bytes 36872 | tf_op jit(solution)/shard_map/ppermute | solution.py:31
  142.2 3.8 %collective-permute-start.22 = (f32[520,256]{1,0:T(8,128)S(1)}, f32[520,256]{1,0:T(8,128)S(1)}, u32[]{:S(2)}, u32[]{:S(2)}) collective-permute-start(f32[520,256]{1,0:T(8,128)S(1)} %get-tuple-element.82.pin_ref), channel_id=1, source_target_pairs={{0,16},{16,0},{32,48},{48,32},{64,80},{80,64},{96,112},{112,96},{1... | collective-permute-start | bytes 1597448 | tf_op jit(solution)/shard_map/ppermute | solution.py:31
  145.3 2.1 %collective-permute-start.23 = (f32[520,256]{1,0:T(8,128)S(1)}, f32[520,256]{1,0:T(8,128)S(1)}, u32[]{:S(2)}, u32[]{:S(2)}) collective-permute-start(f32[520,256]{1,0:T(8,128)S(1)} %get-tuple-element.83.refs_0_), channel_id=1, source_target_pairs={{0,16},{16,0},{32,48},{48,32},{64,80},{80,64},{96,112},{112,96},{1... | collective-permute-start | bytes 1597448 | tf_op jit(solution)/shard_map/ppermute | solution.py:31
  145.9 19.9 %collective-permute-start.21 = (f32[512,512]{1,0:T(8,128)S(1)}, f32[512,512]{1,0:T(8,128)S(1)}, u32[]{:S(2)}, u32[]{:S(2)}) collective-permute-start(f32[512,512]{1,0:T(8,128)S(1)} %column.3.mine_ref), channel_id=1, source_target_pairs={{0,16},{16,0},{32,48},{48,32},{64,80},{80,64},{96,112},{112,96},{1... | collective-permute-start | bytes 3145736 | tf_op jit(solution)/shard_map/ppermute | solution.py:31
  147.5 8.8 %collective-permute-start.24 = (f32[264,256]{1,0:T(8,128)S(1)}, f32[264,256]{1,0:T(8,128)S(1)}, u32[]{:S(2)}, u32[]{:S(2)}) collective-permute-start(f32[264,256]{1,0:T(8,128)S(1)} %get-tuple-element.89), channel_id=1, source_target_pairs={{0,32},{16,48},{32,0},{48,16},{64,96},{80,112},{96,64},{112,80},{1... | collective-permute-start | bytes 811016 | tf_op jit(solution)/shard_map/ppermute | solution.py:31
  147.6 10.1 %collective-permute-start.25 = (f32[264,256]{1,0:T(8,128)S(1)}, f32[264,256]{1,0:T(8,128)S(1)}, u32[]{:S(2)}, u32[]{:S(2)}) collective-permute-start(f32[264,256]{1,0:T(8,128)S(1)} %get-tuple-element.91), channel_id=1, source_target_pairs={{0,96},{16,112},{32,64},{48,80},{64,32},{80,48},{96,0},{112,16},{1... | collective-permute-start | bytes 811016 | tf_op jit(solution)/shard_map/ppermute | solution.py:31
  157.8 6.4 %collective-permute-start.26 = (f32[136,256]{1,0:T(8,128)S(1)}, f32[136,256]{1,0:T(8,128)S(1)}, u32[]{:S(2)}, u32[]{:S(2)}) collective-permute-start(f32[136,256]{1,0:T(8,128)S(1)} %get-tuple-element.93), channel_id=1, source_target_pairs={{0,96},{16,112},{32,64},{48,80},{64,32},{80,48},{96,0},{112,16},{1... | collective-permute-start | bytes 417800 | tf_op jit(solution)/shard_map/ppermute | solution.py:31
  159.3 5.1 %collective-permute-start.27 = (f32[136,256]{1,0:T(8,128)S(1)}, f32[136,256]{1,0:T(8,128)S(1)}, u32[]{:S(2)}, u32[]{:S(2)}) collective-permute-start(f32[136,256]{1,0:T(8,128)S(1)} %get-tuple-element.95), channel_id=1, source_target_pairs={{0,32},{16,48},{32,0},{48,16},{64,96},{80,112},{96,64},{112,80},{1... | collective-permute-start | bytes 417800 | tf_op jit(solution)/shard_map/ppermute | solution.py:31
  164.4 10.0 %collective-permute-start.28 = (f32[64,512]{1,0:T(8,128)S(1)}, f32[64,512]{1,0:T(8,128)S(1)}, u32[]{:S(2)}, u32[]{:S(2)}) collective-permute-start(f32[64,512]{1,0:T(8,128)S(1)} %get-tuple-element.97), channel_id=1, source_target_pairs={{0,128},{16,144},{32,160},{48,176},{64,192},{80,208},{96,224},{112... | collective-permute-start | bytes 393224 | tf_op jit(solution)/shard_map/ppermute | solution.py:31
